TPU v7x, 32 devices: a whole 2x2x4 slice. The times are simulated.
32 devices in a mesh: band: 2 (over x), blk: 16 (over z, y, core).
Axes of the slice: x: 2, y: 2, z: 4, core: 2. Of those that a mesh axis runs over, the one named last changes fastest.
Arguments:
- amps: bfloat16 [2560, 16, 128], P(None, 'blk'), may hold values from -6 to 6
- beam: float32 [2, 2560], P('band'), may hold values from 0.2 to 1
- legendre: bfloat16 [16, 2560, 64], P('blk'), as said below
- m_values: int32 [16], replicated, may hold values from 0 to 2559, as said below
- cycle_order: int32 [64], replicated, may hold values from 0 to 63, each once
- pixel_counts: int32 [64], replicated, may hold values from 512 to 4096, as said below
- inv_noise: float32 [2, 64, 4096], P('band', 'blk'), may hold values from 0.1 to 2
Outputs:
- amps_out: float32 [2560, 16, 128], P('band', 'blk')
Inputs may be any that keep to these rules, and one draw needn't show every extreme that they name: `m_values`: distinct orders; both 0 and 2559 occur. legendre[m, l, s] is zero wherever l < m_values[m]. `pixel_counts`: some cycle has exactly 4096 pixels.
All inputs are finite; a program needn't handle non-finite values.
Results may differ from a plain program's by a relative error of at most 0.0017.
Values may be sent and summed in bfloat16 or wider, within the bound.
No kernel may reach another device: no remote copies, remote signals or barrier semaphores. Data moves between devices by JAX's collectives and lax.ppermute only.
A program may use at most 64 MiB of HBM per device.

v0:
```python
import math

import jax
import jax.numpy as jnp
from jax import lax
from jax.sharding import PartitionSpec as P

PIX = 4096


def cycle_table(order_ids, cycle_id, pixel_count, pixels):
    pixel_idx = jnp.arange(pixels, dtype=jnp.int32)
    product_mod = order_ids[:, None] * pixel_idx[None, :] % pixel_count
    parity = cycle_id % 2
    numerator = (2 * product_mod + order_ids[:, None] * parity) % (2 * pixel_count)
    phase_angle = numerator.astype(jnp.float32) * (
        jnp.float32(math.pi) / pixel_count.astype(jnp.float32)
    )
    inside = (pixel_idx < pixel_count)[None, :]
    norm_scale = lax.rsqrt(pixel_count.astype(jnp.float32))
    cos_part = jnp.where(inside, jnp.cos(phase_angle) * norm_scale, jnp.float32(0.0))
    sin_part = jnp.where(inside, -jnp.sin(phase_angle) * norm_scale, jnp.float32(0.0))
    return jnp.stack([cos_part, sin_part], axis=1).reshape(2 * order_ids.shape[0], pixels)


def cycle_pass(modes_in, phase_table, weights):
    orders = modes_in.shape[0]
    chains = modes_in.shape[1] // 2
    modes_flat = modes_in.reshape(2 * orders, chains)
    pixel_field = lax.dot_general(
        modes_flat, phase_table, (((0,), (0,)), ((), ())), precision=lax.Precision.HIGHEST
    )
    weighted_field = pixel_field * weights[None, :]
    projected = lax.dot_general(
        phase_table, weighted_field, (((1,), (1,)), ((), ())), precision=lax.Precision.HIGHEST
    )
    return projected.reshape(orders, 2 * chains)


def shards(amps, beam, legendre, m_values, cycle_order, pixel_counts, inv_noise):
    gains = beam[0]
    weighted = (amps.astype(jnp.float32) * gains[:, None, None]).astype(jnp.bfloat16)
    synth = jnp.einsum("mlr,lmc->rmc", legendre, weighted, preferred_element_type=jnp.float32)
    cycle_local = lax.all_to_all(synth, "blk", split_axis=0, concat_axis=1, tiled=True)
    cycles_here = inv_noise.shape[1]
    all_cycles = cycle_order.shape[0]
    cycle_ids = lax.dynamic_slice_in_dim(
        cycle_order, lax.axis_index("blk") * cycles_here, cycles_here
    )
    matches = cycle_ids[:, None] == jnp.arange(all_cycles, dtype=jnp.int32)[None, :]
    local_counts = jnp.sum(jnp.where(matches, pixel_counts[None, :], 0), axis=1)

    def cycle_one(packed):
        phase_table = cycle_table(m_values, packed[1], packed[2], PIX)
        return cycle_pass(packed[0], phase_table, packed[3])

    projected = lax.map(cycle_one, (cycle_local, cycle_ids, local_counts, inv_noise[0]))
    proj_half = lax.all_to_all(
        projected.astype(jnp.bfloat16), "blk", split_axis=1, concat_axis=0, tiled=True
    )
    partial_rows = jnp.einsum(
        "mlr,rmc->lmc", legendre, proj_half, preferred_element_type=jnp.float32
    )
    return lax.psum_scatter(
        partial_rows * gains[:, None, None], "band", scatter_dimension=0, tiled=True
    )


def solution(mesh):
    return jax.shard_map(
        shards,
        mesh=mesh,
        in_specs=(
            P(None, "blk", None),
            P("band", None),
            P("blk", None, None),
            P(),
            P(),
            P(),
            P("band", "blk", None),
        ),
        out_specs=P("band", "blk", None),
        check_vma=False,
    )
```

profile of v0, /device:TPU:0, one launch (start us, length us, event | category | flops | bytes accessed | tf_op | source)
XLA Modules:
  0.0 134.3 jit_solution(11867041865204290791)
XLA Ops:
  7.5 2.3 %fusion.12 = f32[128,64]{0,1:T(8,128)} fusion(bf16[2560,1,128]{2,0,1:T(8,128)(2,1)} %param.9, f32[2560]{0:T(1024)S(1)} %reduce, bf16[1,2560,64]{1,2,0:T(8,128)(2,1)S(1)} %copy-done), kind=kOutput, calls=%fused_computation.25 | convolution fusion | flops 42926080 | bytes 1026048 | tf_op jit(solution)/shard_map/mlr,lmc->rmc/dot_general | solution.py:43
  9.8 7.4 %all-to-all-start = ((f32[64,1,128]{2,1,0:T(1,128)}), f32[64,1,128]{2,1,0:T(1,128)S(1)}, u32[]{:S(2)}, u32[]{:S(2)}) async-start(f32[64,1,128]{2,1,0:T(1,128)} %bitcast.7), calls=%async_computation | async-start | bytes 65536 | tf_op jit(solution)/shard_map/all_to_all | solution.py:44
  18.8 5.0 %all-to-all-done = f32[64,1,128]{2,1,0:T(1,128)S(1)} async-done(((f32[64,1,128]{2,1,0:T(1,128)}), f32[64,1,128]{2,1,0:T(1,128)S(1)}, u32[]{:S(2)}, u32[]{:S(2)}) %all-to-all-start) | async-done | bytes 32800 | tf_op jit(solution)/shard_map/all_to_all | solution.py:44
  23.8 70.5 %while.12 = (s32[]{:T(128)}, bf16[4,16,128]{2,0,1:T(4,128)(2,1)S(1)}, s32[4]{0:T(128)S(1)}, s32[16]{0:T(128)}, s32[4]{0:T(128)S(1)}, /*index=5*/f32[4,16,128]{2,...) while((s32[]{:T(128)}, bf16[4,16,128]{2,0,1:T(4,128)(2,1)S(1)}, ...), condition=%wide.region_2.3_spmd, body=%wide.region_1.2_spmd.sunk | while | flops 203296800 | bytes 6955654 | solution.py:57
  30.8 0.9 constant_dynamic-slice_fusion.5
  31.6 6.8 %multiply_select_fusion.3 = (f32[16,1,4096]{2,0,1:T(8,128)S(1)}, f32[16,1,4096]{2,0,1:T(8,128)S(1)}) fusion(f32[]{:T(128)S(6)} %rsqrt.7, f32[]{:T(128)S(6)} %div.7, pred[]{:T(512)S(6)} %lt.114, s32[]{:T(128)S(6)} %select_n.136, s32[16]{0:T(128)S(1)} %broadcast_multiply_fusion.2, pred[]{:T(512)S(6)} %lt.116, s32[]{:T(128)S(6)} %select_n.138, ...), kind=kLoop, calls=%fused_computation.10.clone.1 | loop fusion | flops 1572864 | bytes 528530 | tf_op jit(solution)/shard_map/while/body/eval_jaxpr/jit(_where)/select_n | solution.py:21
  39.3 1.0 convolution_multiply_fusion.2
  40.3 1.0 fusion.32
  48.4 0.9 constant_dynamic-slice_fusion.5
  49.2 6.8 %multiply_select_fusion.3 = (f32[16,1,4096]{2,0,1:T(8,128)S(1)}, f32[16,1,4096]{2,0,1:T(8,128)S(1)}) fusion(f32[]{:T(128)S(6)} %rsqrt.7, f32[]{:T(128)S(6)} %div.7, pred[]{:T(512)S(6)} %lt.114, s32[]{:T(128)S(6)} %select_n.136, s32[16]{0:T(128)S(1)} %broadcast_multiply_fusion.2, pred[]{:T(512)S(6)} %lt.116, s32[]{:T(128)S(6)} %select_n.138, ...), kind=kLoop, calls=%fused_computation.10.clone.1 | loop fusion | flops 1572864 | bytes 528530 | tf_op jit(solution)/shard_map/while/body/eval_jaxpr/jit(_where)/select_n | solution.py:21
  56.9 1.0 convolution_multiply_fusion.2
  57.9 1.0 fusion.32
  66.0 0.9 constant_dynamic-slice_fusion.5
  66.9 6.8 %multiply_select_fusion.3 = (f32[16,1,4096]{2,0,1:T(8,128)S(1)}, f32[16,1,4096]{2,0,1:T(8,128)S(1)}) fusion(f32[]{:T(128)S(6)} %rsqrt.7, f32[]{:T(128)S(6)} %div.7, pred[]{:T(512)S(6)} %lt.114, s32[]{:T(128)S(6)} %select_n.136, s32[16]{0:T(128)S(1)} %broadcast_multiply_fusion.2, pred[]{:T(512)S(6)} %lt.116, s32[]{:T(128)S(6)} %select_n.138, ...), kind=kLoop, calls=%fused_computation.10.clone.1 | loop fusion | flops 1572864 | bytes 528530 | tf_op jit(solution)/shard_map/while/body/eval_jaxpr/jit(_where)/select_n | solution.py:21
  74.5 1.0 convolution_multiply_fusion.2
  75.6 1.0 fusion.32
  83.6 0.9 constant_dynamic-slice_fusion.5
  84.5 6.8 %multiply_select_fusion.3 = (f32[16,1,4096]{2,0,1:T(8,128)S(1)}, f32[16,1,4096]{2,0,1:T(8,128)S(1)}) fusion(f32[]{:T(128)S(6)} %rsqrt.7, f32[]{:T(128)S(6)} %div.7, pred[]{:T(512)S(6)} %lt.114, s32[]{:T(128)S(6)} %select_n.136, s32[16]{0:T(128)S(1)} %broadcast_multiply_fusion.2, pred[]{:T(512)S(6)} %lt.116, s32[]{:T(128)S(6)} %select_n.138, ...), kind=kLoop, calls=%fused_computation.10.clone.1 | loop fusion | flops 1572864 | bytes 528530 | tf_op jit(solution)/shard_map/while/body/eval_jaxpr/jit(_where)/select_n | solution.py:21
  92.1 1.0 convolution_multiply_fusion.2
  93.2 1.0 fusion.32
  94.3 9.1 %all_to_all.33 = bf16[4,16,128]{2,0,1:T(4,128)(2,1)S(1)} all-to-all(bf16[4,16,128]{2,0,1:T(4,128)(2,1)S(1)} %get-tuple-element.95), channel_id=1, replica_groups=mesh['band'=2,'blk'=16] {'blk'}, dimensions={1} | all-to-all | bytes 32768 | tf_op jit(solution)/shard_map/all_to_all | solution.py:58
  103.3 1.4 %fusion.10 = f32[2560,1,128]{0,2,1:T(8,128)} fusion(bf16[64,128]{1,0:T(8,128)(2,1)S(1)} %bitcast.63, f32[2560]{0:T(1024)S(1)} %reduce, bf16[1,2560,64]{1,2,0:T(8,128)(2,1)S(1)} %copy-done), kind=kOutput, calls=%fused_computation.22 | convolution fusion | flops 42270720 | bytes 1665024 | tf_op jit(solution)/shard_map/mlr,rmc->lmc/dot_general | solution.py:61
  104.8 20.6 %reduce-scatter.2.cloned.1.call-done = f32[1280,1,128]{0,2,1:T(8,128)} async-done(((f32[2560,1,128]{0,2,1:T(8,128)}), f32[1280,1,128]{0,2,1:T(8,128)}) %reduce-scatter.2.cloned.1.call-update) | async-done | bytes 655376 | tf_op jit(solution)/shard_map/reduce_scatter | solution.py:64
  125.4 2.0 %copy.29 = f32[1280,1,128]{2,1,0:T(1,128)} copy(f32[1280,1,128]{0,2,1:T(8,128)} %reduce-scatter.2.cloned.1.call-done) | data formatting | bytes 1310720 | tf_op jit(solution)/shard_map/reduce_scatter | solution.py:64
  (53 shorter events, 16.5 us)
Async XLA Ops:
  6.5 1.0 copy-start
  9.8 14.0 %all-to-all-start = ((f32[64,1,128]{2,1,0:T(1,128)}), f32[64,1,128]{2,1,0:T(1,128)S(1)}, u32[]{:S(2)}, u32[]{:S(2)}) async-start(f32[64,1,128]{2,1,0:T(1,128)} %bitcast.7), calls=%async_computation | async-start | bytes 65536 | tf_op jit(solution)/shard_map/all_to_all | solution.py:44
  17.2 108.2 %reduce-scatter.2.cloned.1.call-start = ((), (), s32[]{:S(2)}) async-start(), calls=%async_computation.3 | async-start | bytes 1966080 | tf_op jit(solution)/shard_map/reduce_scatter | solution.py:64
Sparse Core Ops, SparseCore 0:
  104.9 20.4 reduce-scatter.1
where the time goes:
time: 135 us; the launch traced here: 134 us
  other arithmetic  34.4 us (25%)
  waiting for transfers between devices  25.6 us (19%)
  loops' own time  17.8 us (13%)
  local copies, waits for them, and re-layouts  14.9 us (11%)
  between operations  13.4 us (10%)
  matrix products  11.6 us (9%)
  blocking collectives  9.07 us (7%)
  starting transfers between devices  7.42 us (5%)
    select_n x4, other arithmetic, cycle_table(): jnp.where(inside, jnp.cos(phase_angle) * norm_scale, jnp.float32(0.0))  27.4 us
    reduce_scatter x1, waiting for transfers between devices, shards(): lax.psum_scatter(partial_rows * gains[:, None, None], 'band', scatter_dim...  20.6 us
    another operation x1, loops' own time, shards(): lax.map(cycle_one, (cycle_local, cycle_ids, local_counts, inv_noise[0]))  17.8 us
    all_to_all x1, blocking collectives, shards(): lax.all_to_all(projected.astype(jnp.bfloat16), 'blk', split_axis=1, conca...  9.07 us
    dynamic_slice x16, local copies, waits for them, and re-layouts, shards(): lax.map(cycle_one, (cycle_local, cycle_ids, local_counts, inv_noise[0]))  8.14 us
    all_to_all x1, starting transfers between devices, shards(): lax.all_to_all(synth, 'blk', split_axis=0, concat_axis=1, tiled=True)  7.38 us
    all_to_all x1, waiting for transfers between devices, shards(): lax.all_to_all(synth, 'blk', split_axis=0, concat_axis=1, tiled=True)  5 us
    dot_general x4, matrix products, cycle_pass(): lax.dot_general(modes_flat, phase_table, (((0,), (0,)), ((), ())), precis...  4.1 us
  transfers between devices with their start and end apart: 2, of which 2 were waited for; matrix products, arithmetic and copies ran while one was open for 1% of the time, Pallas kernels for 0%

commit v1 on v0

v1 whole, which is shorter than its diff:
```python
import functools
import math

import jax
import jax.numpy as jnp
from jax import lax
from jax.experimental import pallas as pl
from jax.experimental.pallas import tpu as pltpu
from jax.sharding import PartitionSpec as P

LANES = 128
VMEM = pltpu.CompilerParams(vmem_limit_bytes=48 * 1024 * 1024)
NT = (((1,), (1,)), ((), ()))


def synth_kernel(amps_ref, beam_ref, leg_ref, out_ref, weighted):
    chunks = beam_ref.shape[0]
    gains = beam_ref[...].T
    for k in range(chunks):
        rows = pl.ds(k * LANES, LANES)
        product = amps_ref[rows, :].astype(jnp.float32) * gains[:, k : k + 1]
        weighted[rows, :] = product.astype(jnp.bfloat16)
    out_ref[...] = jnp.dot(leg_ref[...], weighted[...], preferred_element_type=jnp.float32)


def mod_exact(value, modulus):
    quotient = (value.astype(jnp.float32) / modulus.astype(jnp.float32)).astype(jnp.int32)
    left = value - quotient * modulus
    left = jnp.where(left < 0, left + modulus, left)
    return jnp.where(left >= modulus, left - modulus, left)


def cos_sin(numer, count):
    countf = count.astype(jnp.float32)
    quarter = ((2 * numer + (count >> 1)).astype(jnp.float32) / countf).astype(jnp.int32)
    rest = (2 * numer - quarter * count).astype(jnp.float32)
    angle = rest * (jnp.float32(math.pi / 2) / countf)
    square = angle * angle
    sin = angle * (
        1.0 + square * (-1.0 / 6 + square * (1.0 / 120 + square * (-1.0 / 5040 + square * (1.0 / 362880))))
    )
    cos = 1.0 + square * (
        -0.5 + square * (1.0 / 24 + square * (-1.0 / 720 + square * (1.0 / 40320 - square * (1.0 / 3628800))))
    )
    odd = (quarter & 1) == 1
    cos_out = jnp.where(odd, sin, cos)
    sin_out = jnp.where(odd, cos, sin)
    cos_out = jnp.where(((quarter + 1) & 2) == 2, -cos_out, cos_out)
    sin_out = jnp.where((quarter & 2) == 2, -sin_out, sin_out)
    return cos_out, sin_out


def gram_kernel(start_ref, order_ref, cycle_ref, count_ref, noise_ref, gram_ref, high, low):
    cycles, pixels = noise_ref.shape
    orders = order_ref.shape[0]
    rows = orders * cycles
    start = start_ref[0]
    row = lax.broadcasted_iota(jnp.int32, (rows, LANES), 0)
    lane = lax.broadcasted_iota(jnp.int32, (rows, LANES), 1)
    slot = row % cycles
    count = jnp.zeros((rows, LANES), jnp.int32)
    parity = jnp.zeros((rows, LANES), jnp.int32)
    for i in range(cycles):
        cycle = cycle_ref[start + i]
        count = jnp.where(slot == i, count_ref[cycle], count)
        parity = jnp.where(slot == i, cycle & 1, parity)
    order = jnp.zeros((rows, LANES), jnp.int32)
    for m in range(orders):
        order = jnp.where(row // cycles == m, order_ref[m], order)
    fine_c, fine_s = cos_sin(mod_exact(2 * order * lane, 2 * count), count)
    coarse = 2 * LANES * order * (lane & (pixels // LANES - 1)) + order * parity
    coarse_c, coarse_s = cos_sin(mod_exact(coarse, 2 * count), count)
    norm = lax.rsqrt(count.astype(jnp.float32))
    fine_c, fine_s = fine_c * norm, fine_s * norm
    coarse_s = -coarse_s

    pixel = lax.broadcasted_iota(jnp.int32, (cycles, pixels), 1)
    inside = pixel < count[:cycles, :1]
    root = jnp.sqrt(jnp.where(inside, noise_ref[...], 0.0))
    reps = max(8 // cycles, 1)
    root = jnp.concatenate([root] * reps, axis=0)
    period = root.shape[0]

    step = 2
    total = jnp.zeros((2 * rows, 4 * rows), jnp.float32)
    for block in range(pixels // LANES // step):
        for j in range(block * step, (block + 1) * step):
            cols = slice(j * LANES, (j + 1) * LANES)
            here = jnp.concatenate([root[:, cols]] * (rows // period), axis=0)
            a_c, a_s = coarse_c[:, j : j + 1], coarse_s[:, j : j + 1]
            for c, value in enumerate((a_c * fine_c + a_s * fine_s, a_s * fine_c - a_c * fine_s)):
                value = value * here
                top = value.astype(jnp.bfloat16)
                high[c * rows : (c + 1) * rows, cols] = top
                low[c * rows : (c + 1) * rows, cols] = (value - top.astype(jnp.float32)).astype(jnp.bfloat16)
        cols = slice(block * step * LANES, (block + 1) * step * LANES)
        top = high[:, cols]
        both = jnp.concatenate([top, low[:, cols]], axis=0)
        total = total + lax.dot_general(top, both, NT, preferred_element_type=jnp.float32)
    cross = total[:, 2 * rows :]
    gram = total[:, : 2 * rows] + cross + cross.T
    row = lax.broadcasted_iota(jnp.int32, gram.shape, 0)
    col = lax.broadcasted_iota(jnp.int32, gram.shape, 1)
    gram_ref[...] = jnp.where(row % cycles == col % cycles, gram, 0.0)


def apply_kernel(bands, gram_ref, modes_ref, out_ref):
    rows, width = modes_ref.shape
    chains = width // 2
    modes = modes_ref[...]
    stacked = jnp.concatenate([modes[:, :chains], modes[:, chains:]], axis=0)
    result = jnp.dot(
        gram_ref[...], stacked, precision=lax.Precision.HIGHEST, preferred_element_type=jnp.float32
    )
    half = jnp.concatenate([result[:rows], result[rows:]], axis=1).astype(jnp.bfloat16)
    for b in range(bands):
        out_ref[b * rows : (b + 1) * rows, :] = half


def analysis_kernel(bands, gain_ref, leg_ref, half_ref, out_ref):
    cycles, degrees = leg_ref.shape
    width = half_ref.shape[1]
    halves = [half_ref[b * cycles : (b + 1) * cycles, :] for b in range(bands)]
    right = jnp.concatenate(halves, axis=1)
    gains = gain_ref[...].T
    size = 256 if degrees % 256 == 0 else degrees
    for at in range(0, degrees, size):
        product = lax.dot_general(
            leg_ref[:, at : at + size],
            right,
            (((0,), (0,)), ((), ())),
            preferred_element_type=jnp.float32,
        )
        total = gains[at : at + size, 0:1] * product[:, :width]
        for b in range(1, bands):
            total = total + gains[at : at + size, b : b + 1] * product[:, b * width : (b + 1) * width]
        out_ref[at : at + size, :] = total


def shards(bands, amps, beam, legendre, m_values, cycle_order, pixel_counts, inv_noise):
    degrees, _, width = amps.shape
    cycles = legendre.shape[2]
    cycles_here = inv_noise.shape[1]
    orders = m_values.shape[0]
    rows = orders * cycles_here
    part = degrees // bands
    leg = jnp.swapaxes(legendre[0], 0, 1)
    smem = pl.BlockSpec(memory_space=pltpu.SMEM)
    vmem = pl.BlockSpec(memory_space=pltpu.VMEM)

    synth = pl.pallas_call(
        synth_kernel,
        out_shape=jax.ShapeDtypeStruct((cycles, width), jnp.float32),
        in_specs=[vmem] * 3,
        out_specs=vmem,
        scratch_shapes=[pltpu.VMEM((degrees, width), jnp.bfloat16)],
        compiler_params=VMEM,
    )(amps[:, 0, :], beam.reshape(degrees // LANES, LANES), leg)
    modes = lax.all_to_all(synth, "blk", split_axis=0, concat_axis=0, tiled=True)

    start = (lax.axis_index("blk") * cycles_here).astype(jnp.int32).reshape(1)
    gram = pl.pallas_call(
        gram_kernel,
        out_shape=jax.ShapeDtypeStruct((2 * rows, 2 * rows), jnp.float32),
        in_specs=[smem] * 4 + [vmem],
        out_specs=vmem,
        scratch_shapes=[pltpu.VMEM((2 * rows, inv_noise.shape[2]), jnp.bfloat16)] * 2,
        compiler_params=VMEM,
    )(start, m_values, cycle_order, pixel_counts, inv_noise[0])

    half = pl.pallas_call(
        functools.partial(apply_kernel, bands),
        out_shape=jax.ShapeDtypeStruct((bands * rows, width), jnp.bfloat16),
        in_specs=[vmem] * 2,
        out_specs=vmem,
        compiler_params=VMEM,
    )(gram, modes)
    half = lax.all_to_all(half, ("band", "blk"), split_axis=0, concat_axis=0, tiled=True)

    gains = lax.all_to_all(beam.reshape(bands, part), "band", split_axis=0, concat_axis=0, tiled=True)
    leg_part = lax.dynamic_slice_in_dim(leg, lax.axis_index("band") * part, part, axis=1)
    out = pl.pallas_call(
        functools.partial(analysis_kernel, bands),
        out_shape=jax.ShapeDtypeStruct((part, width), jnp.float32),
        in_specs=[vmem] * 3,
        out_specs=vmem,
        compiler_params=VMEM,
    )(gains, leg_part, half)
    return out[:, None, :]


def solution(mesh):
    return jax.shard_map(
        functools.partial(shards, mesh.shape["band"]),
        mesh=mesh,
        in_specs=(
            P(None, "blk", None),
            P("band", None),
            P("blk", None, None),
            P(),
            P(),
            P(),
            P("band", "blk", None),
        ),
        out_specs=P("band", "blk", None),
        check_vma=False,
    )
```

time: 135 us -> 36.4 us (0.27)
  other arithmetic: 34.4 us -> 0.73 us
  loops' own time: 17.8 us -> 0 us
  waiting for transfers between devices: 25.6 us -> 8.06 us
  between operations: 13.4 us -> 0.12 us
  local copies, waits for them, and re-layouts: 14.9 us -> 2.1 us
  matrix products: 11.6 us -> 0 us
  Pallas kernels: 0 us -> 5.28 us
  blocking collectives: 9.07 us -> 14 us
  starting transfers between devices: 7.42 us -> 5.8 us
    select_n x4 -> x0, other arithmetic: 27.4 us -> none  [cycle_table(): jnp.where(inside, jnp.cos(phase_angle) * norm_scale, jnp.float32(0.0))]
    reduce_scatter x1 -> x0, waiting for transfers between devices: 20.6 us -> none  [shards(): lax.psum_scatter(partial_rows * gains[:, None, None], 'band', scatter_dim...]
    another operation x1 -> x0, loops' own time: 17.8 us -> none  [shards(): lax.map(cycle_one, (cycle_local, cycle_ids, local_counts, inv_noise[0]))]
    dot_general x10 -> x0, matrix products: 11.6 us -> none  [the longest x4 4.1 us: cycle_pass(): lax.dot_general(modes_flat, phase_table, (((0,), (0,)), ((), ())), precis...]
    dynamic_slice x17 -> x1, local copies, waits for them, and re-layouts: 8.87 us -> 0.02 us  [shards(): lax.dynamic_slice_in_dim(leg, lax.axis_index('band') * part, part, axis=1)]
    pallas_call x0 -> x4, Pallas kernels: none -> 5.28 us  [the longest x1 1.94 us: shards(): pl.pallas_call(gram_kernel, out_shape=jax.ShapeDtypeStruct((2 * rows, 2 *...]
    all_to_all x1, blocking collectives: 9.07 us -> 14 us  [shards(): lax.all_to_all(synth, 'blk', split_axis=0, concat_axis=0, tiled=True)]
    all_to_all x1 -> x2, waiting for transfers between devices: 5 us -> 8.06 us  [the longest x1 7.2 us: shards(): lax.all_to_all(half, ('band', 'blk'), split_axis=0, concat_axis=0, tiled=...]
  transfers between devices with their start and end apart: 2 -> 2, of which waited for: 2 -> 2; matrix products, arithmetic and copies ran while one was open for 1% -> 0% of each run, Pallas kernels for 0% -> 8%
where the time goes in v1:
time: 36.4 us; the launch traced here: 36 us
  blocking collectives  14 us (38%)
  waiting for transfers between devices  8.06 us (22%)
  starting transfers between devices  5.8 us (16%)
  Pallas kernels  5.28 us (15%)
  local copies, waits for them, and re-layouts  2.1 us (6%)
  other arithmetic  0.73 us (2%)
    all_to_all x1, blocking collectives, shards(): lax.all_to_all(synth, 'blk', split_axis=0, concat_axis=0, tiled=True)  14 us
    all_to_all x1, waiting for transfers between devices, shards(): lax.all_to_all(half, ('band', 'blk'), split_axis=0, concat_axis=0, tiled=...  7.2 us
    all_to_all x1, starting transfers between devices, shards(): lax.all_to_all(beam.reshape(bands, part), 'band', split_axis=0, concat_ax...  3.23 us
    all_to_all x1, starting transfers between devices, shards(): lax.all_to_all(half, ('band', 'blk'), split_axis=0, concat_axis=0, tiled=...  2.57 us
    unnamed x15, local copies, waits for them, and re-layouts  2.08 us
    pallas_call x1, Pallas kernels, shards(): pl.pallas_call(gram_kernel, out_shape=jax.ShapeDtypeStruct((2 * rows, 2 *...  1.94 us
    pallas_call x1, Pallas kernels, shards(): pl.pallas_call(functools.partial(analysis_kernel, bands), out_shape=jax.S...  1.55 us
    pallas_call x1, Pallas kernels, shards(): pl.pallas_call(functools.partial(apply_kernel, bands), out_shape=jax.Shap...  0.95 us
  transfers between devices with their start and end apart: 2, of which 2 were waited for; matrix products, arithmetic and copies ran while one was open for 0% of the time, Pallas kernels for 8%

profile of v1, /device:TPU:0, one launch (start us, length us, event | category | flops | bytes accessed | tf_op | source)
XLA Modules:
  0.0 36.0 jit_solution(15265534849502206675)
XLA Ops:
  0.0 0.7 %reduce = f32[2560]{0:T(1024)S(1)} reduce(f32[1,2560]{1,0:T(1,128)} %param.8, f32[]{:T(128)} %constant.22), dimensions={0}, to_apply=%param.8.reduce_sub_computation | reduce | bytes 20484 | tf_op args[1]
  0.7 0.0 copy-start
  0.7 1.0 %copy-done = bf16[1,2560,64]{1,2,0:T(8,128)(2,1)S(1)} copy-done((bf16[1,2560,64]{1,2,0:T(8,128)(2,1)S(1)}, bf16[1,2560,64]{1,2,0:T(8,128)(2,1)}, u32[]{:S(2)}) %copy-start) | copy-done | bytes 327704
  1.7 0.0 copy-start.2
  1.7 1.1 %copy-done.2 = bf16[2560,1,128]{2,0,1:T(8,128)(2,1)S(1)} copy-done((bf16[2560,1,128]{2,0,1:T(8,128)(2,1)S(1)}, bf16[2560,1,128]{2,0,1:T(8,128)(2,1)}, u32[]{:S(2)}) %copy-start.2) | copy-done | bytes 655384
  2.8 0.0 copy-start.3
  2.8 0.0 copy-start.4
  2.8 0.0 copy-start.5
  2.8 0.0 copy-start.6
  2.8 0.8 %shard_map.74 = f32[64,128]{1,0:T(8,128)S(1)} custom-call(bf16[2560,128]{1,0:T(8,128)(2,1)S(1)} %bitcast.23, f32[20,128]{1,0:T(8,128)S(1)} %bitcast.28, bf16[64,2560]{1,0:T(8,128)(2,1)S(1)} %bitcast.22), custom_call_target="tpu_custom_call" | custom-call | tf_op jit(solution)/shard_map/pallas_call | solution.py:151
  3.6 0.0 copy-start.1
  3.7 14.0 %all_to_all.33 = f32[16,4,128]{2,1,0:T(4,128)S(1)} all-to-all(f32[16,4,128]{2,1,0:T(4,128)S(1)} %bitcast.24), channel_id=1, replica_groups=mesh['band'=2,'blk'=16] {'blk'}, dimensions={0} | all-to-all | bytes 65536 | tf_op jit(solution)/shard_map/all_to_all | solution.py:159
  17.6 3.2 %all-to-all-start = ((f32[2,1,1280]{2,1,0:T(1,128)}), f32[2,1,1280]{2,1,0:T(1,128)S(1)}, u32[]{:S(2)}, u32[]{:S(2)}) async-start(f32[2,1,1280]{2,1,0:T(1,128)} %bitcast), calls=%async_computation | async-start | bytes 20480 | tf_op jit(solution)/shard_map/all_to_all | solution.py:180
  20.9 0.0 copy-done.3
  20.9 0.0 copy-done.4
  20.9 0.0 copy-done.5
  20.9 0.0 copy-done.6
  20.9 1.9 %shard_map.73.gram_ref = f32[128,128]{1,0:T(8,128)S(1)} custom-call(s32[1]{0:T(128)} %bitcast.3.start_ref, s32[16]{0:T(128)S(1)} %copy-done.4, s32[64]{0:T(128)S(1)} %copy-done.5, s32[64]{0:T(128)S(1)} %copy-done.6, f32[4,4096]{1,0:T(4,128)S(1)} %bitcast.27), custom_call_target="tpu_custom_call" | custom-call | tf_op jit(solution)/shard_map/pallas_call | solution.py:162
  22.8 1.0 %shard_map.75 = bf16[128,128]{1,0:T(8,128)(2,1)} custom-call(f32[128,128]{1,0:T(8,128)S(1)} %shard_map.73.gram_ref, f32[64,128]{1,0:T(8,128)S(1)} %bitcast.25), custom_call_target="tpu_custom_call" | custom-call | tf_op jit(solution)/shard_map/pallas_call | solution.py:171
  23.8 0.9 %all-to-all-done = f32[2,1,1280]{2,1,0:T(1,128)S(1)} async-done(((f32[2,1,1280]{2,1,0:T(1,128)}), f32[2,1,1280]{2,1,0:T(1,128)S(1)}, u32[]{:S(2)}, u32[]{:S(2)}) %all-to-all-start) | async-done | bytes 10272 | tf_op jit(solution)/shard_map/all_to_all | solution.py:180
  24.7 2.6 %all-to-all-start.2 = ((bf16[32,4,128]{2,1,0:T(4,128)(2,1)}), bf16[32,4,128]{2,1,0:T(4,128)(2,1)S(1)}, u32[]{:S(2)}, u32[]{:S(2)}) async-start(bf16[32,4,128]{2,1,0:T(4,128)(2,1)} %bitcast.10), calls=%async_computation.2 | async-start | bytes 65536 | tf_op jit(solution)/shard_map/all_to_all | solution.py:178
  27.2 0.0 copy-done.1
  27.3 7.2 %all-to-all-done.2 = bf16[32,4,128]{2,1,0:T(4,128)(2,1)S(1)} async-done(((bf16[32,4,128]{2,1,0:T(4,128)(2,1)}), bf16[32,4,128]{2,1,0:T(4,128)(2,1)S(1)}, u32[]{:S(2)}, u32[]{:S(2)}) %all-to-all-start.2) | async-done | bytes 32800 | tf_op jit(solution)/shard_map/all_to_all | solution.py:178
  34.5 1.6 %shard_map.76 = f32[1280,128]{1,0:T(8,128)} custom-call(f32[2,1280]{1,0:T(2,128)S(1)} %bitcast.29, bf16[64,1280]{1,0:T(8,128)(2,1)S(1)} %dynamic-slice_bitcast_fusion.leg_ref, bf16[128,128]{1,0:T(8,128)(2,1)S(1)} %bitcast.26), custom_call_target="tpu_custom_call" | custom-call | tf_op jit(solution)/shard_map/pallas_call | solution.py:182
  (2 shorter events, 0.0 us)
Async XLA Ops:
  0.7 1.0 %copy-start = (bf16[1,2560,64]{1,2,0:T(8,128)(2,1)S(1)}, bf16[1,2560,64]{1,2,0:T(8,128)(2,1)}, u32[]{:S(2)}) copy-start(bf16[1,2560,64]{1,2,0:T(8,128)(2,1)} %param.9) | copy-start | bytes 983044
  1.7 1.1 %copy-start.2 = (bf16[2560,1,128]{2,0,1:T(8,128)(2,1)S(1)}, bf16[2560,1,128]{2,0,1:T(8,128)(2,1)}, u32[]{:S(2)}) copy-start(bf16[2560,1,128]{2,0,1:T(8,128)(2,1)} %param.7) | copy-start | bytes 1966084
  2.8 18.1 %copy-start.3 = (f32[1,4,4096]{2,1,0:T(4,128)S(1)}, f32[1,4,4096]{2,1,0:T(4,128)}, u32[]{:S(2)}) copy-start(f32[1,4,4096]{2,1,0:T(4,128)} %param.13) | copy-start | bytes 196612
  2.8 18.1 %copy-start.4 = (s32[16]{0:T(128)S(1)}, s32[16]{0:T(128)}, u32[]{:S(2)}) copy-start(s32[16]{0:T(128)} %order_ref.1) | copy-start | bytes 196
  2.8 18.1 %copy-start.5 = (s32[64]{0:T(128)S(1)}, s32[64]{0:T(128)}, u32[]{:S(2)}) copy-start(s32[64]{0:T(128)} %cycle_ref.1) | copy-start | bytes 772
  2.8 18.1 %copy-start.6 = (s32[64]{0:T(128)S(1)}, s32[64]{0:T(128)}, u32[]{:S(2)}) copy-start(s32[64]{0:T(128)} %count_ref.1) | copy-start | bytes 772
  3.6 23.6 %copy-start.1 = (bf16[1,2560,64]{1,2,0:T(8,128)(2,1)S(1)}, bf16[1,2560,64]{1,2,0:T(8,128)(2,1)}, u32[]{:S(2)}) copy-start(bf16[1,2560,64]{1,2,0:T(8,128)(2,1)} %param.9) | copy-start | bytes 983044
  17.6 7.0 %all-to-all-start = ((f32[2,1,1280]{2,1,0:T(1,128)}), f32[2,1,1280]{2,1,0:T(1,128)S(1)}, u32[]{:S(2)}, u32[]{:S(2)}) async-start(f32[2,1,1280]{2,1,0:T(1,128)} %bitcast), calls=%async_computation | async-start | bytes 20480 | tf_op jit(solution)/shard_map/all_to_all | solution.py:180
  24.7 9.8 %all-to-all-start.2 = ((bf16[32,4,128]{2,1,0:T(4,128)(2,1)}), bf16[32,4,128]{2,1,0:T(4,128)(2,1)S(1)}, u32[]{:S(2)}, u32[]{:S(2)}) async-start(bf16[32,4,128]{2,1,0:T(4,128)(2,1)} %bitcast.10), calls=%async_computation.2 | async-start | bytes 65536 | tf_op jit(solution)/shard_map/all_to_all | solution.py:178

commit v2 on v1

--- a/solution.py
+++ b/solution.py
@@ -9,18 +9,51 @@
 from jax.sharding import PartitionSpec as P
 
 LANES = 128
+SLAB = 512
 VMEM = pltpu.CompilerParams(vmem_limit_bytes=48 * 1024 * 1024)
 NT = (((1,), (1,)), ((), ()))
 
 
-def synth_kernel(amps_ref, beam_ref, leg_ref, out_ref, weighted):
-    chunks = beam_ref.shape[0]
-    gains = beam_ref[...].T
+def synth_kernel(bands, amps_hbm, beam_hbm, leg_hbm, out_ref, own_ref, amps, beam, leg, weighted, padded, sems):
+    degrees = amps.shape[0]
+    chunks = amps_hbm.shape[0] // SLAB
+    cycles = leg.shape[0]
+    band, blk = lax.axis_index("band"), lax.axis_index("blk")
+    copies = [pltpu.make_async_copy(beam_hbm, beam, sems.at[0])]
     for k in range(chunks):
-        rows = pl.ds(k * LANES, LANES)
-        product = amps_ref[rows, :].astype(jnp.float32) * gains[:, k : k + 1]
-        weighted[rows, :] = product.astype(jnp.bfloat16)
-    out_ref[...] = jnp.dot(leg_ref[...], weighted[...], preferred_element_type=jnp.float32)
+        at = pl.ds(k * SLAB, SLAB)
+        copies.append(pltpu.make_async_copy(amps_hbm.at[at, :], amps.at[at, :], sems.at[1 + 2 * k]))
+        copies.append(pltpu.make_async_copy(leg_hbm.at[:, at], leg.at[:, at], sems.at[2 + 2 * k]))
+    for copy in copies:
+        copy.start()
+    copies[0].wait()
+    gains = jnp.concatenate(
+        [beam[0:1, k * LANES : (k + 1) * LANES] for k in range(degrees // LANES)], axis=0
+    ).T
+    part = degrees // bands
+    lines = -(-part // LANES)
+    padded[...] = jnp.zeros_like(padded)
+    for p in range(bands):
+        for t in range(lines):
+            size = min(LANES, part - t * LANES)
+            first = p * part + t * LANES
+            padded[p * lines + t : p * lines + t + 1, :size] = beam[0:1, first : first + size]
+    rows = cycles // lax.axis_size("blk")
+    for p in range(bands):
+        piece = padded[pl.ds(p * lines + blk * rows, rows), :]
+        out_ref[p * cycles : (p + 1) * cycles, :] = jnp.concatenate([piece] * (cycles // rows), axis=0)
+    own_ref[...] = padded[pl.ds(band * lines, lines), :]
+    total = None
+    for k in range(chunks):
+        copies[1 + 2 * k].wait()
+        copies[2 + 2 * k].wait()
+        for j in range(k * SLAB, (k + 1) * SLAB, LANES):
+            product = amps[j : j + LANES, :].astype(jnp.float32) * gains[:, j // LANES : j // LANES + 1]
+            weighted[j : j + LANES, :] = product.astype(jnp.bfloat16)
+        at = slice(k * SLAB, (k + 1) * SLAB)
+        add = jnp.dot(leg[:, at], weighted[at, :], preferred_element_type=jnp.float32)
+        total = add if total is None else total + add
+    out_ref[pl.ds(pl.multiple_of(band * cycles, 8), cycles), :] = total
 
 
 def mod_exact(value, modulus):
@@ -101,40 +134,58 @@
     gram = total[:, : 2 * rows] + cross + cross.T
     row = lax.broadcasted_iota(jnp.int32, gram.shape, 0)
     col = lax.broadcasted_iota(jnp.int32, gram.shape, 1)
-    gram_ref[...] = jnp.where(row % cycles == col % cycles, gram, 0.0)
+    gram = jnp.where(row % cycles == col % cycles, gram, 0.0)
+    top = gram.astype(jnp.bfloat16)
+    rest = (gram - top.astype(jnp.float32)).astype(jnp.bfloat16)
+    gram_ref[...] = jnp.concatenate([top, top, rest], axis=1)
 
 
 def apply_kernel(bands, gram_ref, modes_ref, out_ref):
-    rows, width = modes_ref.shape
+    rows = gram_ref.shape[0] // 2
+    width = modes_ref.shape[1]
     chains = width // 2
-    modes = modes_ref[...]
+    cycles = modes_ref.shape[0] // bands
+    modes = modes_ref[pl.ds(pl.multiple_of(lax.axis_index("band") * cycles, 8), cycles), :]
     stacked = jnp.concatenate([modes[:, :chains], modes[:, chains:]], axis=0)
-    result = jnp.dot(
-        gram_ref[...], stacked, precision=lax.Precision.HIGHEST, preferred_element_type=jnp.float32
-    )
+    top = stacked.astype(jnp.bfloat16)
+    rest = (stacked - top.astype(jnp.float32)).astype(jnp.bfloat16)
+    right = jnp.concatenate([top, rest, top], axis=0)
+    result = jnp.dot(gram_ref[...], right, preferred_element_type=jnp.float32)
     half = jnp.concatenate([result[:rows], result[rows:]], axis=1).astype(jnp.bfloat16)
     for b in range(bands):
         out_ref[b * rows : (b + 1) * rows, :] = half
 
 
-def analysis_kernel(bands, gain_ref, leg_ref, half_ref, out_ref):
-    cycles, degrees = leg_ref.shape
-    width = half_ref.shape[1]
-    halves = [half_ref[b * cycles : (b + 1) * cycles, :] for b in range(bands)]
-    right = jnp.concatenate(halves, axis=1)
-    gains = gain_ref[...].T
+def matrix_kernel(bands, modes_ref, own_ref, leg_ref, out_ref):
+    cycles, part = leg_ref.shape
+    lines = own_ref.shape[0]
+    band = lax.axis_index("band")
+    columns = []
+    for b in range(bands):
+        sent = modes_ref[b * cycles : b * cycles + lines, :]
+        columns.append(jnp.where(band == b, own_ref[...], sent).T)
+    for t in range(lines):
+        size = min(LANES, part - t * LANES)
+        turned = leg_ref[:, t * LANES : t * LANES + size].astype(jnp.float32).T
+        scaled = [turned * column[:size, t : t + 1] for column in columns]
+        scaled = jnp.concatenate(scaled, axis=1)
+        top = scaled.astype(jnp.bfloat16)
+        rest = (scaled - top.astype(jnp.float32)).astype(jnp.bfloat16)
+        out_ref[t * LANES : t * LANES + size, :] = jnp.concatenate([top, rest], axis=1)
+
+
+def analysis_kernel(matrix_ref, half_ref, out_hbm, out, sems):
+    degrees = out.shape[0]
     size = 256 if degrees % 256 == 0 else degrees
-    for at in range(0, degrees, size):
-        product = lax.dot_general(
-            leg_ref[:, at : at + size],
-            right,
-            (((0,), (0,)), ((), ())),
-            preferred_element_type=jnp.float32,
-        )
-        total = gains[at : at + size, 0:1] * product[:, :width]
-        for b in range(1, bands):
-            total = total + gains[at : at + size, b : b + 1] * product[:, b * width : (b + 1) * width]
-        out_ref[at : at + size, :] = total
+    right = jnp.concatenate([half_ref[...]] * 2, axis=0)
+    copies = []
+    for k in range(degrees // size):
+        at = pl.ds(k * size, size)
+        out[at, :] = jnp.dot(matrix_ref[at, :], right, preferred_element_type=jnp.float32)
+        copies.append(pltpu.make_async_copy(out.at[at, :], out_hbm.at[at, :], sems.at[k]))
+        copies[-1].start()
+    for copy in copies:
+        copy.wait()
 
 
 def shards(bands, amps, beam, legendre, m_values, cycle_order, pixel_counts, inv_noise):
@@ -148,24 +199,44 @@
     smem = pl.BlockSpec(memory_space=pltpu.SMEM)
     vmem = pl.BlockSpec(memory_space=pltpu.VMEM)
 
-    synth = pl.pallas_call(
-        synth_kernel,
-        out_shape=jax.ShapeDtypeStruct((cycles, width), jnp.float32),
-        in_specs=[vmem] * 3,
-        out_specs=vmem,
-        scratch_shapes=[pltpu.VMEM((degrees, width), jnp.bfloat16)],
-        compiler_params=VMEM,
-    )(amps[:, 0, :], beam.reshape(degrees // LANES, LANES), leg)
-    modes = lax.all_to_all(synth, "blk", split_axis=0, concat_axis=0, tiled=True)
+    hbm = pl.BlockSpec(memory_space=pltpu.HBM)
+    lines = -(-part // LANES)
+    slabs = degrees // SLAB
+    sent, own = pl.pallas_call(
+        functools.partial(synth_kernel, bands),
+        out_shape=[
+            jax.ShapeDtypeStruct((bands * cycles, width), jnp.float32),
+            jax.ShapeDtypeStruct((lines, LANES), jnp.float32),
+        ],
+        in_specs=[hbm] * 3,
+        out_specs=[vmem] * 2,
+        scratch_shapes=[
+            pltpu.VMEM((degrees, width), jnp.bfloat16),
+            pltpu.VMEM((1, degrees), jnp.float32),
+            pltpu.VMEM((cycles, degrees), jnp.bfloat16),
+            pltpu.VMEM((degrees, width), jnp.bfloat16),
+            pltpu.VMEM((bands * lines + cycles, LANES), jnp.float32),
+            pltpu.SemaphoreType.DMA((1 + 2 * slabs,)),
+        ],
+        compiler_params=pltpu.CompilerParams(vmem_limit_bytes=127 * 512 * 1024),
+        cost_estimate=pl.CostEstimate(
+            flops=2 * degrees * cycles * width, transcendentals=0, bytes_accessed=2 * degrees * (cycles + width)
+        ),
+    )(amps[:, 0, :], beam, leg)
+    modes = lax.all_to_all(sent, ("band", "blk"), split_axis=0, concat_axis=0, tiled=True)
 
     start = (lax.axis_index("blk") * cycles_here).astype(jnp.int32).reshape(1)
+    pixels = inv_noise.shape[2]
     gram = pl.pallas_call(
         gram_kernel,
-        out_shape=jax.ShapeDtypeStruct((2 * rows, 2 * rows), jnp.float32),
+        out_shape=jax.ShapeDtypeStruct((2 * rows, 6 * rows), jnp.bfloat16),
         in_specs=[smem] * 4 + [vmem],
         out_specs=vmem,
-        scratch_shapes=[pltpu.VMEM((2 * rows, inv_noise.shape[2]), jnp.bfloat16)] * 2,
-        compiler_params=VMEM,
+        scratch_shapes=[pltpu.VMEM((2 * rows, pixels), jnp.bfloat16)] * 2,
+        compiler_params=VMEM,
+        cost_estimate=pl.CostEstimate(
+            flops=16 * rows * rows * pixels, transcendentals=0, bytes_accessed=8 * rows * pixels
+        ),
     )(start, m_values, cycle_order, pixel_counts, inv_noise[0])
 
     half = pl.pallas_call(
@@ -175,17 +246,28 @@
         out_specs=vmem,
         compiler_params=VMEM,
     )(gram, modes)
+    half, modes, own, leg = lax.optimization_barrier((half, modes, own, leg))
     half = lax.all_to_all(half, ("band", "blk"), split_axis=0, concat_axis=0, tiled=True)
 
-    gains = lax.all_to_all(beam.reshape(bands, part), "band", split_axis=0, concat_axis=0, tiled=True)
     leg_part = lax.dynamic_slice_in_dim(leg, lax.axis_index("band") * part, part, axis=1)
-    out = pl.pallas_call(
-        functools.partial(analysis_kernel, bands),
-        out_shape=jax.ShapeDtypeStruct((part, width), jnp.float32),
+    matrix = pl.pallas_call(
+        functools.partial(matrix_kernel, bands),
+        out_shape=jax.ShapeDtypeStruct((part, 2 * bands * cycles), jnp.bfloat16),
         in_specs=[vmem] * 3,
         out_specs=vmem,
         compiler_params=VMEM,
-    )(gains, leg_part, half)
+        cost_estimate=pl.CostEstimate(
+            flops=8 * part * bands * cycles, transcendentals=0, bytes_accessed=4 * part * bands * cycles
+        ),
+    )(modes, own, leg_part)
+    out = pl.pallas_call(
+        analysis_kernel,
+        out_shape=jax.ShapeDtypeStruct((part, width), jnp.float32),
+        in_specs=[vmem] * 2,
+        out_specs=hbm,
+        scratch_shapes=[pltpu.VMEM((part, width), jnp.float32), pltpu.SemaphoreType.DMA((max(part // 256, 1),))],
+        compiler_params=VMEM,
+    )(matrix, half)
     return out[:, None, :]
 
 

time: 36.4 us -> 30.1 us (0.83)
  blocking collectives: 14 us -> 0 us
  starting transfers between devices: 5.8 us -> 9.87 us
  Pallas kernels: 5.28 us -> 8.54 us
  waiting for transfers between devices: 8.06 us -> 9.93 us
  local copies, waits for them, and re-layouts: 2.1 us -> 1.35 us
  other arithmetic: 0.73 us -> 0 us
    all_to_all x1 -> x0, blocking collectives: 14 us -> none  [shards(): lax.all_to_all(synth, 'blk', split_axis=0, concat_axis=0, tiled=True)]
    all_to_all x1, starting transfers between devices: 3.23 us -> 7.3 us  [shards(): lax.all_to_all(sent, ('band', 'blk'), split_axis=0, concat_axis=0, tiled=...]
    all_to_all x1, waiting for transfers between devices: 0.86 us -> 4.76 us  [shards(): lax.all_to_all(sent, ('band', 'blk'), split_axis=0, concat_axis=0, tiled=...]
    pallas_call x3 -> x4, Pallas kernels: 4.33 us -> 7.61 us  [the longest x1 3.22 us: shards(): pl.pallas_call(functools.partial(synth_kernel, bands), out_shape=[jax.Sha...]
    all_to_all x1, waiting for transfers between devices: 7.2 us -> 5.16 us  [shards(): lax.all_to_all(half, ('band', 'blk'), split_axis=0, concat_axis=0, tiled=...]
    unnamed x15 -> x12, local copies, waits for them, and re-layouts: 2.08 us -> 1.33 us
    unnamed x1 -> x0, other arithmetic: 0.73 us -> none
  transfers between devices with their start and end apart: 2 -> 2, of which waited for: 2 -> 2; matrix products, arithmetic and copies ran while one was open for 0% -> 0% of each run, Pallas kernels for 8% -> 11%
where the time goes in v2:
time: 30.1 us; the launch traced here: 29.8 us
  waiting for transfers between devices  9.93 us (33%)
  starting transfers between devices  9.87 us (33%)
  Pallas kernels  8.54 us (28%)
  local copies, waits for them, and re-layouts  1.35 us (4%)
    all_to_all x1, starting transfers between devices, shards(): lax.all_to_all(sent, ('band', 'blk'), split_axis=0, concat_axis=0, tiled=...  7.3 us
    all_to_all x1, waiting for transfers between devices, shards(): lax.all_to_all(half, ('band', 'blk'), split_axis=0, concat_axis=0, tiled=...  5.16 us
    all_to_all x1, waiting for transfers between devices, shards(): lax.all_to_all(sent, ('band', 'blk'), split_axis=0, concat_axis=0, tiled=...  4.76 us
    pallas_call x1, Pallas kernels, shards(): pl.pallas_call(functools.partial(synth_kernel, bands), out_shape=[jax.Sha...  3.22 us
    all_to_all x1, starting transfers between devices, shards(): lax.all_to_all(half, ('band', 'blk'), split_axis=0, concat_axis=0, tiled=...  2.57 us
    pallas_call x1, Pallas kernels, shards(): pl.pallas_call(gram_kernel, out_shape=jax.ShapeDtypeStruct((2 * rows, 6 *...  1.94 us
    pallas_call x1, Pallas kernels, shards(): pl.pallas_call(functools.partial(matrix_kernel, bands), out_shape=jax.Sha...  1.37 us
    unnamed x12, local copies, waits for them, and re-layouts  1.33 us
  transfers between devices with their start and end apart: 2, of which 2 were waited for; matrix products, arithmetic and copies ran while one was open for 0% of the time, Pallas kernels for 11%

profile of v2, /device:TPU:0, one launch (start us, length us, event | category | flops | bytes accessed | tf_op | source)
XLA Modules:
  0.0 29.8 jit_solution(11745510558559051373)
XLA Ops:
  0.0 3.2 %shard_map.74 = (f32[128,128]{1,0:T(8,128)}, f32[10,128]{1,0:T(8,128)}) custom-call(bf16[2560,128]{1,0:T(8,128)(2,1)} %bitcast.19, f32[1,2560]{1,0:T(1,128)} %beam_hbm.1, bf16[64,2560]{1,0:T(8,128)(2,1)} %bitcast.17), custom_call_target="tpu_custom_call" | custom-call | flops 41943040 | bytes 983040 | tf_op jit(solution)/shard_map/pallas_call | solution.py:205
  3.2 0.0 copy-start.1
  3.2 7.3 %all-to-all-start = ((f32[32,4,128]{2,1,0:T(4,128)}), f32[32,4,128]{2,1,0:T(4,128)S(1)}, u32[]{:S(2)}, u32[]{:S(2)}) async-start(f32[32,4,128]{2,1,0:T(4,128)} %bitcast.20), calls=%async_computation | async-start | bytes 131072 | tf_op jit(solution)/shard_map/all_to_all | solution.py:226
  10.6 0.0 copy-start.2
  10.6 0.0 copy-start.3
  10.6 0.0 copy-start.4
  10.6 0.0 copy-done.1
  10.6 0.6 %copy-done.2 = s32[16]{0:T(128)S(1)} copy-done((s32[16]{0:T(128)S(1)}, s32[16]{0:T(128)}, u32[]{:S(2)}) %copy-start.2) | copy-done | bytes 88
  11.2 0.0 copy-done.3
  11.2 0.0 copy-done.4
  11.3 0.0 copy-start.5
  11.3 1.9 %shard_map.73.gram_ref = bf16[128,384]{1,0:T(8,128)(2,1)S(1)} custom-call(s32[1]{0:T(128)} %bitcast.start_ref, s32[16]{0:T(128)S(1)} %copy-done.2, s32[64]{0:T(128)S(1)} %copy-done.3, s32[64]{0:T(128)S(1)} %copy-done.4, f32[4,4096]{1,0:T(4,128)S(1)} %bitcast.16), custom_call_target="tpu_custom_call" | custom-call | flops 268435456 | bytes 2097152 | tf_op jit(solution)/shard_map/pallas_call | solution.py:230
  13.2 4.8 %all-to-all-done = f32[32,4,128]{2,1,0:T(4,128)S(1)} async-done(((f32[32,4,128]{2,1,0:T(4,128)}), f32[32,4,128]{2,1,0:T(4,128)S(1)}, u32[]{:S(2)}, u32[]{:S(2)}) %all-to-all-start) | async-done | bytes 65568 | tf_op jit(solution)/shard_map/all_to_all | solution.py:226
  18.0 0.9 %shard_map.75 = bf16[128,128]{1,0:T(8,128)(2,1)} custom-call(bf16[128,384]{1,0:T(8,128)(2,1)S(1)} %shard_map.73.gram_ref, f32[128,128]{1,0:T(8,128)S(1)} %bitcast.13), custom_call_target="tpu_custom_call" | custom-call | tf_op jit(solution)/shard_map/pallas_call | solution.py:242
  18.9 2.6 %all-to-all-start.1 = ((bf16[32,4,128]{2,1,0:T(4,128)(2,1)}), bf16[32,4,128]{2,1,0:T(4,128)(2,1)S(1)}, u32[]{:S(2)}, u32[]{:S(2)}) async-start(bf16[32,4,128]{2,1,0:T(4,128)(2,1)} %bitcast.7), calls=%async_computation.1 | async-start | bytes 65536 | tf_op jit(solution)/shard_map/all_to_all | solution.py:250
  21.5 0.0 copy-done.5
  21.5 0.0 copy-start
  21.5 0.7 %copy-done = f32[10,128]{1,0:T(8,128)S(1)} copy-done((f32[10,128]{1,0:T(8,128)S(1)}, f32[10,128]{1,0:T(8,128)}, u32[]{:S(2)}) %copy-start) | copy-done | bytes 5144
  22.2 1.4 %shard_map.76.matrix_ref = bf16[1280,256]{1,0:T(8,128)(2,1)S(1)} custom-call(f32[128,128]{1,0:T(8,128)S(1)} %bitcast.14, f32[10,128]{1,0:T(8,128)S(1)} %copy-done, bf16[64,1280]{1,0:T(8,128)(2,1)S(1)} %constant_dynamic-slice_fusion.leg_ref), custom_call_target="tpu_custom_call" | custom-call | flops 1310720 | bytes 655360 | tf_op jit(solution)/shard_map/pallas_call | solution.py:253
  23.6 5.2 %all-to-all-done.1 = bf16[32,4,128]{2,1,0:T(4,128)(2,1)S(1)} async-done(((bf16[32,4,128]{2,1,0:T(4,128)(2,1)}), bf16[32,4,128]{2,1,0:T(4,128)(2,1)S(1)}, u32[]{:S(2)}, u32[]{:S(2)}) %all-to-all-start.1) | async-done | bytes 32800 | tf_op jit(solution)/shard_map/all_to_all | solution.py:250
  28.7 1.1 %shard_map.77 = f32[1280,128]{1,0:T(8,128)} custom-call(bf16[1280,256]{1,0:T(8,128)(2,1)S(1)} %shard_map.76.matrix_ref, bf16[128,128]{1,0:T(8,128)(2,1)S(1)} %bitcast.15), custom_call_target="tpu_custom_call" | custom-call | tf_op jit(solution)/shard_map/pallas_call | solution.py:263
  (1 shorter events, 0.0 us)
Async XLA Ops:
  3.2 7.4 %copy-start.1 = (f32[1,4,4096]{2,1,0:T(4,128)S(1)}, f32[1,4,4096]{2,1,0:T(4,128)}, u32[]{:S(2)}) copy-start(f32[1,4,4096]{2,1,0:T(4,128)} %param.13) | copy-start | bytes 196612
  3.2 14.7 %all-to-all-start = ((f32[32,4,128]{2,1,0:T(4,128)}), f32[32,4,128]{2,1,0:T(4,128)S(1)}, u32[]{:S(2)}, u32[]{:S(2)}) async-start(f32[32,4,128]{2,1,0:T(4,128)} %bitcast.20), calls=%async_computation | async-start | bytes 131072 | tf_op jit(solution)/shard_map/all_to_all | solution.py:226
  10.6 0.7 %copy-start.2 = (s32[16]{0:T(128)S(1)}, s32[16]{0:T(128)}, u32[]{:S(2)}) copy-start(s32[16]{0:T(128)} %order_ref.1) | copy-start | bytes 196
  10.6 0.7 %copy-start.3 = (s32[64]{0:T(128)S(1)}, s32[64]{0:T(128)}, u32[]{:S(2)}) copy-start(s32[64]{0:T(128)} %cycle_ref.1) | copy-start | bytes 772
  10.6 0.7 %copy-start.4 = (s32[64]{0:T(128)S(1)}, s32[64]{0:T(128)}, u32[]{:S(2)}) copy-start(s32[64]{0:T(128)} %count_ref.1) | copy-start | bytes 772
  11.3 10.2 %copy-start.5 = (bf16[1,2560,64]{1,2,0:T(8,128)(2,1)S(1)}, bf16[1,2560,64]{1,2,0:T(8,128)(2,1)}, u32[]{:S(2)}) copy-start(bf16[1,2560,64]{1,2,0:T(8,128)(2,1)} %param.9) | copy-start | bytes 983044
  18.9 9.8 %all-to-all-start.1 = ((bf16[32,4,128]{2,1,0:T(4,128)(2,1)}), bf16[32,4,128]{2,1,0:T(4,128)(2,1)S(1)}, u32[]{:S(2)}, u32[]{:S(2)}) async-start(bf16[32,4,128]{2,1,0:T(4,128)(2,1)} %bitcast.7), calls=%async_computation.1 | async-start | bytes 65536 | tf_op jit(solution)/shard_map/all_to_all | solution.py:250
  21.5 0.7 %copy-start = (f32[10,128]{1,0:T(8,128)S(1)}, f32[10,128]{1,0:T(8,128)}, u32[]{:S(2)}) copy-start(f32[10,128]{1,0:T(8,128)} %get-tuple-element.14.own_ref) | copy-start | bytes 15364

commit v3 on v2

v3 whole, which is shorter than its diff:
```python
import functools
import math

import jax
import jax.numpy as jnp
from jax import lax
from jax.experimental import pallas as pl
from jax.experimental.pallas import tpu as pltpu
from jax.sharding import PartitionSpec as P

LANES = 128
SLAB = 512
EXTRA = 8
TERMS = 3
VMEM = pltpu.CompilerParams(vmem_limit_bytes=48 * 1024 * 1024)
NT = (((1,), (1,)), ((), ()))


def member_order(blks):
    quarter = blks // 4
    order = [q * quarter + i for q in (2, 3, 1, 0) for i in reversed(range(quarter))]
    return [k for k in order if k % 2 == 1] + [k for k in order if k % 2 == 0]


def synth_kernel(blks, amps_hbm, beam_hbm, leg_hbm, out_ref, amps, beam, leg, weighted, sems):
    degrees = amps.shape[0]
    chunks = amps_hbm.shape[0] // SLAB
    copies = [pltpu.make_async_copy(beam_hbm, beam, sems.at[0])]
    for k in range(chunks):
        at = pl.ds(k * SLAB, SLAB)
        copies.append(pltpu.make_async_copy(amps_hbm.at[at, :], amps.at[at, :], sems.at[1 + 2 * k]))
        copies.append(pltpu.make_async_copy(leg_hbm.at[:, at], leg.at[:, at], sems.at[2 + 2 * k]))
    for copy in copies:
        copy.start()
    copies[0].wait()
    gains = jnp.concatenate(
        [beam[0:1, k * LANES : (k + 1) * LANES] for k in range(degrees // LANES)], axis=0
    ).T
    total = None
    for k in range(chunks):
        copies[1 + 2 * k].wait()
        copies[2 + 2 * k].wait()
        for j in range(k * SLAB, (k + 1) * SLAB, LANES):
            product = amps[j : j + LANES, :].astype(jnp.float32) * gains[:, j // LANES : j // LANES + 1]
            weighted[j : j + LANES, :] = product.astype(jnp.bfloat16)
        at = slice(k * SLAB, (k + 1) * SLAB)
        add = jnp.dot(leg[:, at], weighted[at, :], preferred_element_type=jnp.float32)
        total = add if total is None else total + add
    pair = 2 * total.shape[0] // blks
    for g, k in enumerate(member_order(blks)):
        out_ref[g * pair : (g + 1) * pair, :] = total[k // 2 * pair : (k // 2 + 1) * pair, :]


def mod_exact(value, modulus):
    quotient = (value.astype(jnp.float32) / modulus.astype(jnp.float32)).astype(jnp.int32)
    left = value - quotient * modulus
    left = jnp.where(left < 0, left + modulus, left)
    return jnp.where(left >= modulus, left - modulus, left)


def cos_sin(numer, count):
    countf = count.astype(jnp.float32)
    quarter = ((2 * numer + (count >> 1)).astype(jnp.float32) / countf).astype(jnp.int32)
    rest = (2 * numer - quarter * count).astype(jnp.float32)
    angle = rest * (jnp.float32(math.pi / 2) / countf)
    square = angle * angle
    sin = angle * (
        1.0 + square * (-1.0 / 6 + square * (1.0 / 120 + square * (-1.0 / 5040 + square * (1.0 / 362880))))
    )
    cos = 1.0 + square * (
        -0.5 + square * (1.0 / 24 + square * (-1.0 / 720 + square * (1.0 / 40320 - square * (1.0 / 3628800))))
    )
    odd = (quarter & 1) == 1
    cos_out = jnp.where(odd, sin, cos)
    sin_out = jnp.where(odd, cos, sin)
    cos_out = jnp.where(((quarter + 1) & 2) == 2, -cos_out, cos_out)
    sin_out = jnp.where((quarter & 2) == 2, -sin_out, sin_out)
    return cos_out, sin_out


def gram_kernel(blks, bands, order_ref, cycle_ref, count_ref, noise_ref, beam_ref, keep_ref, give_ref, extra_ref, high, low, whole, lists):
    cycles, pixels = noise_ref.shape
    orders = order_ref.shape[0]
    rows = orders * cycles
    blk = lax.axis_index("blk")
    start = blk * cycles
    row = lax.broadcasted_iota(jnp.int32, (rows, LANES), 0)
    lane = lax.broadcasted_iota(jnp.int32, (rows, LANES), 1)
    slot = row % cycles
    count = jnp.zeros((rows, LANES), jnp.int32)
    parity = jnp.zeros((rows, LANES), jnp.int32)
    for i in range(cycles):
        cycle = cycle_ref[start + i]
        count = jnp.where(slot == i, count_ref[cycle], count)
        parity = jnp.where(slot == i, cycle & 1, parity)
    order = jnp.zeros((rows, LANES), jnp.int32)
    for g, k in enumerate(member_order(blks)):
        order = jnp.where(row // cycles == g, order_ref[k], order)
    fine_c, fine_s = cos_sin(mod_exact(2 * order * lane, 2 * count), count)
    coarse = 2 * LANES * order * (lane & (pixels // LANES - 1)) + order * parity
    coarse_c, coarse_s = cos_sin(mod_exact(coarse, 2 * count), count)
    norm = lax.rsqrt(count.astype(jnp.float32))
    fine_c, fine_s = fine_c * norm, fine_s * norm
    coarse_s = -coarse_s

    pixel = lax.broadcasted_iota(jnp.int32, (cycles, pixels), 1)
    inside = pixel < count[:cycles, :1]
    root = jnp.sqrt(jnp.where(inside, noise_ref[...], 0.0))
    reps = max(8 // cycles, 1)
    root = jnp.concatenate([root] * reps, axis=0)
    period = root.shape[0]

    step = 2
    total = jnp.zeros((2 * rows, 4 * rows), jnp.float32)
    for block in range(pixels // LANES // step):
        for j in range(block * step, (block + 1) * step):
            cols = slice(j * LANES, (j + 1) * LANES)
            here = jnp.concatenate([root[:, cols]] * (rows // period), axis=0)
            a_c, a_s = coarse_c[:, j : j + 1], coarse_s[:, j : j + 1]
            for c, value in enumerate((a_c * fine_c + a_s * fine_s, a_s * fine_c - a_c * fine_s)):
                value = value * here
                top = value.astype(jnp.bfloat16)
                rest = (value - top.astype(jnp.float32)).astype(jnp.bfloat16)
                for p in range(2):
                    to = slice(p * rows + c * (rows // 2), p * rows + (c + 1) * (rows // 2))
                    of = slice(p * (rows // 2), (p + 1) * (rows // 2))
                    high[to, cols] = top[of]
                    low[to, cols] = rest[of]
        cols = slice(block * step * LANES, (block + 1) * step * LANES)
        top = high[:, cols]
        both = jnp.concatenate([top, low[:, cols]], axis=0)
        total = total + lax.dot_general(top, both, NT, preferred_element_type=jnp.float32)
    cross = total[:, 2 * rows :]
    gram = total[:, : 2 * rows] + cross + cross.T
    row = lax.broadcasted_iota(jnp.int32, gram.shape, 0)
    col = lax.broadcasted_iota(jnp.int32, gram.shape, 1)
    gram = jnp.where(row % cycles == col % cycles, gram, 0.0)
    top = gram.astype(jnp.bfloat16)
    rest = (gram - top.astype(jnp.float32)).astype(jnp.bfloat16)
    whole[...] = jnp.concatenate([top, top, rest], axis=1)
    mine = pl.multiple_of((1 - blk % 2) * rows, 16)
    keep_ref[...] = whole[pl.ds(mine, rows), :]
    give_ref[...] = whole[pl.ds(pl.multiple_of(rows - mine, 16), rows), :]

    part = beam_ref.shape[1] // bands
    lines = -(-part // LANES)
    lists[...] = jnp.zeros_like(lists)
    for p in range(bands):
        for t in range(lines):
            size = min(LANES, part - t * LANES)
            first = p * part + t * LANES
            value = beam_ref[0:1, first : first + size]
            for term in range(TERMS):
                top = value.astype(jnp.bfloat16).astype(jnp.float32)
                at = p * (blks // 2) * EXTRA + term * lines + t
                lists[at : at + 1, :size] = top
                value = value - top
        at = pl.multiple_of((p * (blks // 2) + blk // 2) * EXTRA, EXTRA)
        extra_ref[p * EXTRA : (p + 1) * EXTRA, :] = lists[pl.ds(at, EXTRA), :]


def apply_kernel(bands, keep_ref, got_ref, modes_ref, extra_ref, out_ref):
    rows = keep_ref.shape[0]
    pair, width = EXTRA, modes_ref.shape[1]
    chains = width // 2
    first = lax.axis_index("blk") % 2 == 0
    keep, got = keep_ref[...], got_ref[...]
    modes = modes_ref[...].reshape(rows // pair, 2, pair, width)
    even, odd = modes[:, 0], modes[:, 1]
    near = lax.broadcasted_iota(jnp.int32, even.shape, 1) < pair // 2
    halves = []
    for e in range(2):
        if e == 0:
            x = jnp.where(near, even, pltpu.roll(odd, pair // 2, 1))
            matrix = jnp.where(first, keep, got)
        else:
            x = jnp.where(near, pltpu.roll(even, pair // 2, 1), odd)
            matrix = jnp.where(first, got, keep)
        x = x.reshape(rows, width)
        stacked = []
        for p in range(2):
            block = x[p * (rows // 2) : (p + 1) * (rows // 2)]
            stacked += [block[:, :chains], block[:, chains:]]
        stacked = jnp.concatenate(stacked, axis=0)
        top = stacked.astype(jnp.bfloat16)
        rest = (stacked - top.astype(jnp.float32)).astype(jnp.bfloat16)
        right = jnp.concatenate([top, rest, top], axis=0)
        result = jnp.dot(matrix, right, preferred_element_type=jnp.float32)
        half = jnp.concatenate([result[: rows // 2], result[rows // 2 :]], axis=1)
        halves.append(half.reshape(rows // 2 // pair, pair, width))
    near = near[: rows // 2 // pair]
    even = jnp.where(near, halves[0], pltpu.roll(halves[1], pair // 2, 1))
    odd = jnp.where(near, pltpu.roll(halves[0], pair // 2, 1), halves[1])
    size = pair + EXTRA
    for j in range(rows // pair):
        half = (even if j % 2 == 0 else odd)[j // 2]
        for b in range(bands):
            at = (j * bands + bands - 1 - b) * size
            piece = jnp.concatenate([half, extra_ref[b * EXTRA : (b + 1) * EXTRA, :]], axis=0)
            out_ref[at : at + size, :] = piece.astype(jnp.bfloat16)


def turn_kernel(leg_ref, out_ref):
    cycles, part = leg_ref.shape
    for t in range(0, part, LANES):
        size = min(LANES, part - t)
        out_ref[t : t + size, :] = leg_ref[:, t : t + size].astype(jnp.float32).T.astype(jnp.bfloat16)


def analysis_kernel(bands, leg_ref, half_ref, out_hbm, out, sems):
    part, cycles = leg_ref.shape
    width = half_ref.shape[1]
    lines = -(-part // LANES)
    size = 2 * EXTRA
    pairs = half_ref.shape[0] // size // bands
    got = half_ref[...].astype(jnp.float32).reshape(pairs, bands, size, width)
    place = [k // 2 for k in member_order(2 * pairs)[:pairs]]
    place = [place.index(p) for p in range(pairs)]
    right, columns = [], []
    for b in range(bands):
        mine = got[:, bands - 1 - b]
        right.append(jnp.concatenate([mine[place[p], :EXTRA] for p in range(pairs)], axis=0))
        used = -(-TERMS * lines // EXTRA)
        terms = jnp.concatenate([mine[place[p], EXTRA:] for p in range(used)], axis=0)
        gains = terms[:lines]
        for term in range(1, TERMS):
            gains = gains + terms[term * lines : (term + 1) * lines]
        columns.append(gains.T)
    right = jnp.concatenate(right, axis=1).astype(jnp.bfloat16)
    copies = []
    for k in range(len(out_sizes(part))):
        first, many = out_sizes(part)[k]
        product = jnp.dot(leg_ref[first : first + many, :], right, preferred_element_type=jnp.float32)
        for t in range(first, first + many, LANES):
            rows = slice(t, min(t + LANES, part))
            here = product[t - first : t - first + LANES]
            total = None
            for b in range(bands):
                add = columns[b][: here.shape[0], t // LANES : t // LANES + 1] * here[:, b * width : (b + 1) * width]
                total = add if total is None else total + add
            out[rows, :] = total
        at = pl.ds(first, many)
        copies.append(pltpu.make_async_copy(out.at[at, :], out_hbm.at[at, :], sems.at[k]))
        copies[-1].start()
    for copy in copies:
        copy.wait()


def out_sizes(part):
    step = 256
    return [(at, min(step, part - at)) for at in range(0, part, step)]


def shards(bands, amps, beam, legendre, m_values, cycle_order, pixel_counts, inv_noise):
    degrees, _, width = amps.shape
    cycles = legendre.shape[2]
    cycles_here = inv_noise.shape[1]
    orders = m_values.shape[0]
    rows = orders * cycles_here
    part = degrees // bands
    leg = jnp.swapaxes(legendre[0], 0, 1)
    smem = pl.BlockSpec(memory_space=pltpu.SMEM)
    vmem = pl.BlockSpec(memory_space=pltpu.VMEM)

    hbm = pl.BlockSpec(memory_space=pltpu.HBM)
    blks = lax.axis_size("blk")
    pair = 2 * cycles_here
    assert orders == blks and blks % 2 == 0 and pair == EXTRA and cycles == cycles_here * blks
    slabs = degrees // SLAB
    sent = pl.pallas_call(
        functools.partial(synth_kernel, blks),
        out_shape=jax.ShapeDtypeStruct((blks * pair, width), jnp.float32),
        in_specs=[hbm] * 3,
        out_specs=vmem,
        scratch_shapes=[
            pltpu.VMEM((degrees, width), jnp.bfloat16),
            pltpu.VMEM((1, degrees), jnp.float32),
            pltpu.VMEM((cycles, degrees), jnp.bfloat16),
            pltpu.VMEM((degrees, width), jnp.bfloat16),
            pltpu.SemaphoreType.DMA((1 + 2 * slabs,)),
        ],
        compiler_params=pltpu.CompilerParams(vmem_limit_bytes=127 * 512 * 1024),
        cost_estimate=pl.CostEstimate(
            flops=2 * degrees * cycles * width, transcendentals=0, bytes_accessed=2 * degrees * (cycles + width)
        ),
    )(amps[:, 0, :], beam, leg)
    modes = lax.all_to_all(
        sent, "blk", split_axis=0, concat_axis=0, tiled=True, axis_index_groups=[member_order(blks)]
    )

    pixels = inv_noise.shape[2]
    keep, give, extra = pl.pallas_call(
        functools.partial(gram_kernel, blks, bands),
        out_shape=[
            jax.ShapeDtypeStruct((rows, 6 * rows), jnp.bfloat16),
            jax.ShapeDtypeStruct((rows, 6 * rows), jnp.bfloat16),
            jax.ShapeDtypeStruct((bands * EXTRA, LANES), jnp.float32),
        ],
        in_specs=[smem] * 3 + [vmem] * 2,
        out_specs=[vmem] * 3,
        scratch_shapes=[pltpu.VMEM((2 * rows, pixels), jnp.bfloat16)] * 2
        + [
            pltpu.VMEM((2 * rows, 6 * rows), jnp.bfloat16),
            pltpu.VMEM((bands * (blks // 2) * EXTRA, LANES), jnp.float32),
        ],
        compiler_params=VMEM,
        cost_estimate=pl.CostEstimate(
            flops=16 * rows * rows * pixels, transcendentals=0, bytes_accessed=8 * rows * pixels
        ),
    )(m_values, cycle_order, pixel_counts, inv_noise[0], beam)
    got = lax.ppermute(give, "blk", [(k, k ^ 1) for k in range(blks)])

    size = pair + EXTRA
    half = pl.pallas_call(
        functools.partial(apply_kernel, bands),
        out_shape=jax.ShapeDtypeStruct((bands * (blks // 2) * size, width), jnp.bfloat16),
        in_specs=[vmem] * 4,
        out_specs=vmem,
        compiler_params=VMEM,
    )(keep, got, modes, extra)
    half, leg = lax.optimization_barrier((half, leg))
    order = member_order(blks)
    groups = [
        [b * blks + k for k in members for b in reversed(range(bands))]
        for members in (order[: blks // 2], order[blks // 2 :])
    ]
    half = lax.all_to_all(
        half, ("band", "blk"), split_axis=0, concat_axis=0, tiled=True, axis_index_groups=groups
    )

    leg_part = lax.dynamic_slice_in_dim(leg, lax.axis_index("band") * part, part, axis=1)
    leg_turned = pl.pallas_call(
        turn_kernel,
        out_shape=jax.ShapeDtypeStruct((part, cycles), jnp.bfloat16),
        in_specs=[vmem],
        out_specs=vmem,
        compiler_params=VMEM,
        cost_estimate=pl.CostEstimate(flops=part * cycles, transcendentals=0, bytes_accessed=4 * part * cycles),
    )(leg_part)
    out = pl.pallas_call(
        functools.partial(analysis_kernel, bands),
        out_shape=jax.ShapeDtypeStruct((part, width), jnp.float32),
        in_specs=[vmem] * 2,
        out_specs=hbm,
        scratch_shapes=[
            pltpu.VMEM((part, width), jnp.float32),
            pltpu.SemaphoreType.DMA((len(out_sizes(part)),)),
        ],
        compiler_params=VMEM,
    )(leg_turned, half)
    return out[:, None, :]


def solution(mesh):
    return jax.shard_map(
        functools.partial(shards, mesh.shape["band"]),
        mesh=mesh,
        in_specs=(
            P(None, "blk", None),
            P("band", None),
            P("blk", None, None),
            P(),
            P(),
            P(),
            P("band", "blk", None),
        ),
        out_specs=P("band", "blk", None),
        check_vma=False,
    )
```

time: 30.1 us -> 27.6 us (0.917)
  waiting for transfers between devices: 9.93 us -> 4.52 us
  starting transfers between devices: 9.87 us -> 14.4 us
  Pallas kernels: 8.54 us -> 7.59 us
  local copies, waits for them, and re-layouts: 1.35 us -> 0.68 us
    all_to_all x1, waiting for transfers between devices: 4.76 us -> 0.01 us  [shards(): lax.all_to_all(sent, 'blk', split_axis=0, concat_axis=0, tiled=True, axis...]
    all_to_all x1, starting transfers between devices: 2.57 us -> 6.27 us  [shards(): lax.all_to_all(half, ('band', 'blk'), split_axis=0, concat_axis=0, tiled=...]
    all_to_all x1, waiting for transfers between devices: 5.16 us -> 3.36 us  [shards(): lax.all_to_all(half, ('band', 'blk'), split_axis=0, concat_axis=0, tiled=...]
    ppermute x0 -> x1, waiting for transfers between devices: none -> 1.17 us  [shards(): got = lax.ppermute(give, 'blk', [(k, k ^ 1) for k in range(blks)])]
    pallas_call x4, Pallas kernels: 7.61 us -> 6.64 us  [the longest x1 3.22 us: shards(): pl.pallas_call(functools.partial(synth_kernel, blks), out_shape=jax.Shape...]
    unnamed x12, local copies, waits for them, and re-layouts: 1.33 us -> 0.66 us
    all_to_all x1, starting transfers between devices: 7.3 us -> 7.97 us  [shards(): lax.all_to_all(sent, 'blk', split_axis=0, concat_axis=0, tiled=True, axis...]
  transfers between devices with their start and end apart: 2 -> 3, of which waited for: 2 -> 2; matrix products, arithmetic and copies ran while one was open for 0% -> 0% of each run, Pallas kernels for 11% -> 8%
where the time goes in v3:
time: 27.6 us; the launch traced here: 27.3 us
  starting transfers between devices  14.4 us (52%)
  Pallas kernels  7.59 us (28%)
  waiting for transfers between devices  4.52 us (16%)
  local copies, waits for them, and re-layouts  0.68 us (2%)
    all_to_all x1, starting transfers between devices, shards(): lax.all_to_all(sent, 'blk', split_axis=0, concat_axis=0, tiled=True, axis...  7.97 us
    all_to_all x1, starting transfers between devices, shards(): lax.all_to_all(half, ('band', 'blk'), split_axis=0, concat_axis=0, tiled=...  6.27 us
    all_to_all x1, waiting for transfers between devices, shards(): lax.all_to_all(half, ('band', 'blk'), split_axis=0, concat_axis=0, tiled=...  3.36 us
    pallas_call x1, Pallas kernels, shards(): pl.pallas_call(functools.partial(synth_kernel, blks), out_shape=jax.Shape...  3.22 us
    pallas_call x1, Pallas kernels, shards(): pl.pallas_call(functools.partial(gram_kernel, blks, bands), out_shape=[ja...  2 us
    pallas_call x1, Pallas kernels, shards(): pl.pallas_call(functools.partial(analysis_kernel, bands), out_shape=jax.S...  1.25 us
    ppermute x1, waiting for transfers between devices, shards(): got = lax.ppermute(give, 'blk', [(k, k ^ 1) for k in range(blks)])  1.17 us
    pallas_call x1, Pallas kernels, shards(): pl.pallas_call(functools.partial(apply_kernel, bands), out_shape=jax.Shap...  0.95 us
  transfers between devices with their start and end apart: 3, of which 2 were waited for; matrix products, arithmetic and copies ran while one was open for 0% of the time, Pallas kernels for 8%

profile of v3, /device:TPU:0, one launch (start us, length us, event | category | flops | bytes accessed | tf_op | source)
XLA Modules:
  0.0 27.3 jit_solution(3549509789488012848)
XLA Ops:
  0.0 3.2 %shard_map.74 = f32[128,128]{1,0:T(8,128)} custom-call(bf16[2560,128]{1,0:T(8,128)(2,1)} %bitcast.17, f32[1,2560]{1,0:T(1,128)} %beam_hbm.1, bf16[64,2560]{1,0:T(8,128)(2,1)} %bitcast.15), custom_call_target="tpu_custom_call" | custom-call | flops 41943040 | bytes 983040 | tf_op jit(solution)/shard_map/pallas_call | solution.py:270
  3.2 0.0 copy-start
  3.2 0.0 copy-start.1
  3.3 8.0 %all-to-all-start = ((f32[16,8,128]{2,1,0:T(8,128)}), f32[16,8,128]{2,1,0:T(8,128)S(1)}, u32[]{:S(2)}, u32[]{:S(2)}) async-start(f32[16,8,128]{2,1,0:T(8,128)} %bitcast.18), calls=%async_computation | async-start | bytes 131072 | tf_op jit(solution)/shard_map/all_to_all | solution.py:287
  11.2 0.0 copy-start.2
  11.2 0.0 copy-start.3
  11.2 0.0 copy-start.4
  11.3 0.0 copy-done
  11.3 0.0 copy-done.1
  11.3 0.6 %copy-done.2 = s32[16]{0:T(128)S(1)} copy-done((s32[16]{0:T(128)S(1)}, s32[16]{0:T(128)}, u32[]{:S(2)}) %copy-start.2) | copy-done | bytes 88
  11.9 0.0 copy-done.3
  11.9 0.0 copy-done.4
  11.9 2.0 %shard_map.73 = (bf16[64,384]{1,0:T(8,128)(2,1)S(1)}, bf16[64,384]{1,0:T(8,128)(2,1)S(1)}, f32[16,128]{1,0:T(8,128)S(1)}) custom-call(s32[16]{0:T(128)S(1)} %copy-done.2, s32[64]{0:T(128)S(1)} %copy-done.3, s32[64]{0:T(128)S(1)} %copy-done.4, f32[4,4096]{1,0:T(4,128)S(1)} %bitcast.14, f32[1,2560]{1,0:T(1,128)S(1)} %copy-done), custom_call_target="tpu_custom_call" | custom-call | flops 268435456 | bytes 2097152 | tf_op jit(solution)/shard_map/pallas_call | solution.py:292
  13.9 0.0 copy-start.5
  13.9 0.1 collective-permute-start
  14.0 1.2 %collective-permute-done.got_ref = bf16[64,384]{1,0:T(8,128)(2,1)S(1)} collective-permute-done((bf16[64,384]{1,0:T(8,128)(2,1)S(1)}, bf16[64,384]{1,0:T(8,128)(2,1)S(1)}, u32[]{:S(2)}, u32[]{:S(2)}) %collective-permute-start) | collective-permute-done | bytes 49184 | tf_op jit(solution)/shard_map/ppermute | solution.py:311
  15.2 0.0 all-to-all-done
  15.2 0.9 %shard_map.75 = bf16[256,128]{1,0:T(8,128)(2,1)} custom-call(bf16[64,384]{1,0:T(8,128)(2,1)S(1)} %get-tuple-element.10.keep_ref, bf16[64,384]{1,0:T(8,128)(2,1)S(1)} %collective-permute-done.got_ref, f32[128,128]{1,0:T(8,128)S(1)} %bitcast.13, f32[16,128]{1,0:T(8,128)S(1)} %get-tuple-element.12.extra_ref), custom_call_target="tpu_custom_call" | custom-call | tf_op jit(solution)/shard_map/pallas_call | solution.py:314
  16.2 6.3 %all-to-all-start.1 = ((bf16[16,16,128]{2,1,0:T(8,128)(2,1)}), bf16[16,16,128]{2,1,0:T(8,128)(2,1)S(1)}, u32[]{:S(2)}, u32[]{:S(2)}) async-start(bf16[16,16,128]{2,1,0:T(8,128)(2,1)} %bitcast.6), calls=%async_computation.1 | async-start | bytes 131072 | tf_op jit(solution)/shard_map/all_to_all | solution.py:327
  22.4 0.0 copy-done.5
  22.5 0.2 shard_map.76.leg_ref
  22.7 3.4 %all-to-all-done.1 = bf16[16,16,128]{2,1,0:T(8,128)(2,1)S(1)} async-done(((bf16[16,16,128]{2,1,0:T(8,128)(2,1)}), bf16[16,16,128]{2,1,0:T(8,128)(2,1)S(1)}, u32[]{:S(2)}, u32[]{:S(2)}) %all-to-all-start.1) | async-done | bytes 65568 | tf_op jit(solution)/shard_map/all_to_all | solution.py:327
  26.0 1.2 %shard_map.77 = f32[1280,128]{1,0:T(8,128)} custom-call(bf16[1280,64]{1,0:T(8,128)(2,1)S(1)} %shard_map.76.leg_ref, bf16[256,128]{1,0:T(8,128)(2,1)S(1)} %bitcast.12), custom_call_target="tpu_custom_call" | custom-call | tf_op jit(solution)/shard_map/pallas_call | solution.py:340
  (1 shorter events, 0.0 us)
Async XLA Ops:
  3.2 8.0 %copy-start = (f32[1,2560]{1,0:T(1,128)S(1)}, f32[1,2560]{1,0:T(1,128)}, u32[]{:S(2)}) copy-start(f32[1,2560]{1,0:T(1,128)} %beam_hbm.1) | copy-start | bytes 30724
  3.2 8.0 %copy-start.1 = (f32[1,4,4096]{2,1,0:T(4,128)S(1)}, f32[1,4,4096]{2,1,0:T(4,128)}, u32[]{:S(2)}) copy-start(f32[1,4,4096]{2,1,0:T(4,128)} %param.13) | copy-start | bytes 196612
  3.3 12.0 %all-to-all-start = ((f32[16,8,128]{2,1,0:T(8,128)}), f32[16,8,128]{2,1,0:T(8,128)S(1)}, u32[]{:S(2)}, u32[]{:S(2)}) async-start(f32[16,8,128]{2,1,0:T(8,128)} %bitcast.18), calls=%async_computation | async-start | bytes 131072 | tf_op jit(solution)/shard_map/all_to_all | solution.py:287
  11.2 0.7 %copy-start.2 = (s32[16]{0:T(128)S(1)}, s32[16]{0:T(128)}, u32[]{:S(2)}) copy-start(s32[16]{0:T(128)} %order_ref.1) | copy-start | bytes 196
  11.2 0.7 %copy-start.3 = (s32[64]{0:T(128)S(1)}, s32[64]{0:T(128)}, u32[]{:S(2)}) copy-start(s32[64]{0:T(128)} %cycle_ref.1) | copy-start | bytes 772
  11.2 0.7 %copy-start.4 = (s32[64]{0:T(128)S(1)}, s32[64]{0:T(128)}, u32[]{:S(2)}) copy-start(s32[64]{0:T(128)} %count_ref.1) | copy-start | bytes 772
  13.9 8.5 %copy-start.5 = (bf16[1,2560,64]{1,2,0:T(8,128)(2,1)S(1)}, bf16[1,2560,64]{1,2,0:T(8,128)(2,1)}, u32[]{:S(2)}) copy-start(bf16[1,2560,64]{1,2,0:T(8,128)(2,1)} %param.9) | copy-start | bytes 983044
  13.9 1.3 %collective-permute-start = (bf16[64,384]{1,0:T(8,128)(2,1)S(1)}, bf16[64,384]{1,0:T(8,128)(2,1)S(1)}, u32[]{:S(2)}, u32[]{:S(2)}) collective-permute-start(bf16[64,384]{1,0:T(8,128)(2,1)S(1)} %get-tuple-element.11), channel_id=1, source_target_pairs={{0,1},{1,0},{2,3},{3,2},{4,5},{5,4},{6,7},{7,6},{8,9},{9,8},{10,11... | collective-permute-start | bytes 147464 | tf_op jit(solution)/shard_map/ppermute | solution.py:311
  16.2 9.8 %all-to-all-start.1 = ((bf16[16,16,128]{2,1,0:T(8,128)(2,1)}), bf16[16,16,128]{2,1,0:T(8,128)(2,1)S(1)}, u32[]{:S(2)}, u32[]{:S(2)}) async-start(bf16[16,16,128]{2,1,0:T(8,128)(2,1)} %bitcast.6), calls=%async_computation.1 | async-start | bytes 131072 | tf_op jit(solution)/shard_map/all_to_all | solution.py:327

commit v4 on v3

--- a/solution.py
+++ b/solution.py
@@ -9,7 +9,7 @@
 from jax.sharding import PartitionSpec as P
 
 LANES = 128
-SLAB = 512
+SLAB = 1280
 EXTRA = 8
 TERMS = 3
 VMEM = pltpu.CompilerParams(vmem_limit_bytes=48 * 1024 * 1024)
@@ -29,23 +29,20 @@
     for k in range(chunks):
         at = pl.ds(k * SLAB, SLAB)
         copies.append(pltpu.make_async_copy(amps_hbm.at[at, :], amps.at[at, :], sems.at[1 + 2 * k]))
-        copies.append(pltpu.make_async_copy(leg_hbm.at[:, at], leg.at[:, at], sems.at[2 + 2 * k]))
+    copies.append(pltpu.make_async_copy(leg_hbm, leg, sems.at[2]))
     for copy in copies:
         copy.start()
     copies[0].wait()
     gains = jnp.concatenate(
         [beam[0:1, k * LANES : (k + 1) * LANES] for k in range(degrees // LANES)], axis=0
     ).T
-    total = None
     for k in range(chunks):
-        copies[1 + 2 * k].wait()
-        copies[2 + 2 * k].wait()
+        copies[1 + k].wait()
         for j in range(k * SLAB, (k + 1) * SLAB, LANES):
             product = amps[j : j + LANES, :].astype(jnp.float32) * gains[:, j // LANES : j // LANES + 1]
             weighted[j : j + LANES, :] = product.astype(jnp.bfloat16)
-        at = slice(k * SLAB, (k + 1) * SLAB)
-        add = jnp.dot(leg[:, at], weighted[at, :], preferred_element_type=jnp.float32)
-        total = add if total is None else total + add
+    copies[-1].wait()
+    total = jnp.dot(leg[...], weighted[...], preferred_element_type=jnp.float32)
     pair = 2 * total.shape[0] // blks
     for g, k in enumerate(member_order(blks)):
         out_ref[g * pair : (g + 1) * pair, :] = total[k // 2 * pair : (k // 2 + 1) * pair, :]
@@ -310,24 +307,6 @@
     )(m_values, cycle_order, pixel_counts, inv_noise[0], beam)
     got = lax.ppermute(give, "blk", [(k, k ^ 1) for k in range(blks)])
 
-    size = pair + EXTRA
-    half = pl.pallas_call(
-        functools.partial(apply_kernel, bands),
-        out_shape=jax.ShapeDtypeStruct((bands * (blks // 2) * size, width), jnp.bfloat16),
-        in_specs=[vmem] * 4,
-        out_specs=vmem,
-        compiler_params=VMEM,
-    )(keep, got, modes, extra)
-    half, leg = lax.optimization_barrier((half, leg))
-    order = member_order(blks)
-    groups = [
-        [b * blks + k for k in members for b in reversed(range(bands))]
-        for members in (order[: blks // 2], order[blks // 2 :])
-    ]
-    half = lax.all_to_all(
-        half, ("band", "blk"), split_axis=0, concat_axis=0, tiled=True, axis_index_groups=groups
-    )
-
     leg_part = lax.dynamic_slice_in_dim(leg, lax.axis_index("band") * part, part, axis=1)
     leg_turned = pl.pallas_call(
         turn_kernel,
@@ -337,6 +316,24 @@
         compiler_params=VMEM,
         cost_estimate=pl.CostEstimate(flops=part * cycles, transcendentals=0, bytes_accessed=4 * part * cycles),
     )(leg_part)
+    size = pair + EXTRA
+    half = pl.pallas_call(
+        functools.partial(apply_kernel, bands),
+        out_shape=jax.ShapeDtypeStruct((bands * (blks // 2) * size, width), jnp.bfloat16),
+        in_specs=[vmem] * 4,
+        out_specs=vmem,
+        compiler_params=VMEM,
+    )(keep, got, modes, extra)
+    half, leg_turned = lax.optimization_barrier((half, leg_turned))
+    order = member_order(blks)
+    groups = [
+        [b * blks + k for k in members for b in reversed(range(bands))]
+        for members in (order[: blks // 2], order[blks // 2 :])
+    ]
+    half = lax.all_to_all(
+        half, ("band", "blk"), split_axis=0, concat_axis=0, tiled=True, axis_index_groups=groups
+    )
+
     out = pl.pallas_call(
         functools.partial(analysis_kernel, bands),
         out_shape=jax.ShapeDtypeStruct((part, width), jnp.float32),

time: 27.6 us -> 25.7 us (0.931)
  blocking collectives: 0 us -> 9.48 us
  starting transfers between devices: 14.4 us -> 8.08 us
  waiting for transfers between devices: 4.52 us -> 0.98 us
  Pallas kernels: 7.59 us -> 6.15 us
    all_to_all x0 -> x1, blocking collectives: none -> 9.48 us  [shards(): lax.all_to_all(half, ('band', 'blk'), split_axis=0, concat_axis=0, tiled=...]
    all_to_all x1 -> x0, starting transfers between devices: 6.27 us -> none  [shards(): lax.all_to_all(half, ('band', 'blk'), split_axis=0, concat_axis=0, tiled=...]
    all_to_all x1 -> x0, waiting for transfers between devices: 3.36 us -> none  [shards(): lax.all_to_all(half, ('band', 'blk'), split_axis=0, concat_axis=0, tiled=...]
    pallas_call x1, Pallas kernels: 3.22 us -> 2.41 us  [shards(): pl.pallas_call(functools.partial(synth_kernel, blks), out_shape=jax.Shape...]
    pallas_call x1, Pallas kernels: 0.95 us -> 0.31 us  [shards(): pl.pallas_call(functools.partial(apply_kernel, bands), out_shape=jax.Shap...]
  transfers between devices with their start and end apart: 3 -> 2, of which waited for: 2 -> 1; matrix products, arithmetic and copies ran while one was open for 0% -> 0% of each run, Pallas kernels for 8% -> 9%
where the time goes in v4:
time: 25.7 us; the launch traced here: 25.4 us
  blocking collectives  9.48 us (37%)
  starting transfers between devices  8.08 us (31%)
  Pallas kernels  6.15 us (24%)
  waiting for transfers between devices  0.98 us (4%)
  local copies, waits for them, and re-layouts  0.67 us (3%)
    all_to_all x1, blocking collectives, shards(): lax.all_to_all(half, ('band', 'blk'), split_axis=0, concat_axis=0, tiled=...  9.48 us
    all_to_all x1, starting transfers between devices, shards(): lax.all_to_all(sent, 'blk', split_axis=0, concat_axis=0, tiled=True, axis...  7.96 us
    pallas_call x1, Pallas kernels, shards(): pl.pallas_call(functools.partial(synth_kernel, blks), out_shape=jax.Shape...  2.41 us
    pallas_call x1, Pallas kernels, shards(): pl.pallas_call(functools.partial(gram_kernel, blks, bands), out_shape=[ja...  2 us
    pallas_call x1, Pallas kernels, shards(): pl.pallas_call(functools.partial(analysis_kernel, bands), out_shape=jax.S...  1.25 us
    ppermute x1, waiting for transfers between devices, shards(): got = lax.ppermute(give, 'blk', [(k, k ^ 1) for k in range(blks)])  0.97 us
    unnamed x12, local copies, waits for them, and re-layouts  0.66 us
  transfers between devices with their start and end apart: 2, of which 1 were waited for; matrix products, arithmetic and copies ran while one was open for 0% of the time, Pallas kernels for 9%

profile of v4, /device:TPU:0, one launch (start us, length us, event | category | flops | bytes accessed | tf_op | source)
XLA Modules:
  0.0 25.4 jit_solution(18024459289189900711)
XLA Ops:
  0.0 2.4 %shard_map.74 = f32[128,128]{1,0:T(8,128)} custom-call(bf16[2560,128]{1,0:T(8,128)(2,1)} %bitcast.21, f32[1,2560]{1,0:T(1,128)} %beam_hbm.1, bf16[64,2560]{1,0:T(8,128)(2,1)} %bitcast.20), custom_call_target="tpu_custom_call" | custom-call | flops 41943040 | bytes 983040 | tf_op jit(solution)/shard_map/pallas_call | solution.py:267
  2.4 0.0 copy-start
  2.4 0.0 copy-start.1
  2.4 8.0 %all-to-all-start = ((f32[16,8,128]{2,1,0:T(8,128)}), f32[16,8,128]{2,1,0:T(8,128)S(1)}, u32[]{:S(2)}, u32[]{:S(2)}) async-start(f32[16,8,128]{2,1,0:T(8,128)} %bitcast.22), calls=%async_computation | async-start | bytes 131072 | tf_op jit(solution)/shard_map/all_to_all | solution.py:284
  10.4 0.0 copy-start.2
  10.4 0.0 copy-start.3
  10.4 0.0 copy-start.4
  10.4 0.0 copy-done
  10.4 0.0 copy-done.1
  10.5 0.6 %copy-done.2 = s32[16]{0:T(128)S(1)} copy-done((s32[16]{0:T(128)S(1)}, s32[16]{0:T(128)}, u32[]{:S(2)}) %copy-start.2) | copy-done | bytes 88
  11.1 0.0 copy-done.3
  11.1 0.0 copy-done.4
  11.1 0.0 copy-start.5
  11.1 2.0 %shard_map.73 = (bf16[64,384]{1,0:T(8,128)(2,1)S(1)}, bf16[64,384]{1,0:T(8,128)(2,1)S(1)}, f32[16,128]{1,0:T(8,128)S(1)}) custom-call(s32[16]{0:T(128)S(1)} %copy-done.2, s32[64]{0:T(128)S(1)} %copy-done.3, s32[64]{0:T(128)S(1)} %copy-done.4, f32[4,4096]{1,0:T(4,128)S(1)} %bitcast.19, f32[1,2560]{1,0:T(1,128)S(1)} %copy-done), custom_call_target="tpu_custom_call" | custom-call | flops 268435456 | bytes 2097152 | tf_op jit(solution)/shard_map/pallas_call | solution.py:289
  13.1 0.1 collective-permute-start
  13.2 0.0 copy-done.5
  13.2 0.2 shard_map.76.leg_ref
  13.4 1.0 %collective-permute-done.got_ref = bf16[64,384]{1,0:T(8,128)(2,1)S(1)} collective-permute-done((bf16[64,384]{1,0:T(8,128)(2,1)S(1)}, bf16[64,384]{1,0:T(8,128)(2,1)S(1)}, u32[]{:S(2)}, u32[]{:S(2)}) %collective-permute-start) | collective-permute-done | bytes 49184 | tf_op jit(solution)/shard_map/ppermute | solution.py:308
  14.4 0.0 all-to-all-done
  14.4 0.3 %shard_map.75 = bf16[256,128]{1,0:T(8,128)(2,1)S(1)} custom-call(bf16[64,384]{1,0:T(8,128)(2,1)S(1)} %get-tuple-element.10.keep_ref, bf16[64,384]{1,0:T(8,128)(2,1)S(1)} %collective-permute-done.got_ref, f32[128,128]{1,0:T(8,128)S(1)} %bitcast.17, f32[16,128]{1,0:T(8,128)S(1)} %get-tuple-element.12.extra_ref), custom_call_target="tpu_custom_call" | custom-call | tf_op jit(solution)/shard_map/pallas_call | solution.py:320
  14.7 9.5 %all_to_all.22 = bf16[16,16,128]{2,1,0:T(8,128)(2,1)S(1)} all-to-all(bf16[16,16,128]{2,1,0:T(8,128)(2,1)S(1)} %bitcast.18), channel_id=1, replica_groups={{27,11,25,9,31,15,29,13,23,7,21,5,19,3,17,1},{26,10,24,8,30,14,28,12,22..., dimensions={0} | all-to-all | bytes 131072 | tf_op jit(solution)/shard_map/all_to_all | solution.py:333
  24.2 1.3 %shard_map.77 = f32[1280,128]{1,0:T(8,128)} custom-call(bf16[1280,64]{1,0:T(8,128)(2,1)S(1)} %shard_map.76.leg_ref, bf16[256,128]{1,0:T(8,128)(2,1)S(1)} %bitcast.16), custom_call_target="tpu_custom_call" | custom-call | tf_op jit(solution)/shard_map/pallas_call | solution.py:337
  (1 shorter events, 0.0 us)
Async XLA Ops:
  2.4 8.0 %copy-start = (f32[1,2560]{1,0:T(1,128)S(1)}, f32[1,2560]{1,0:T(1,128)}, u32[]{:S(2)}) copy-start(f32[1,2560]{1,0:T(1,128)} %beam_hbm.1) | copy-start | bytes 30724
  2.4 8.0 %copy-start.1 = (f32[1,4,4096]{2,1,0:T(4,128)S(1)}, f32[1,4,4096]{2,1,0:T(4,128)}, u32[]{:S(2)}) copy-start(f32[1,4,4096]{2,1,0:T(4,128)} %param.13) | copy-start | bytes 196612
  2.4 11.9 %all-to-all-start = ((f32[16,8,128]{2,1,0:T(8,128)}), f32[16,8,128]{2,1,0:T(8,128)S(1)}, u32[]{:S(2)}, u32[]{:S(2)}) async-start(f32[16,8,128]{2,1,0:T(8,128)} %bitcast.22), calls=%async_computation | async-start | bytes 131072 | tf_op jit(solution)/shard_map/all_to_all | solution.py:284
  10.4 0.7 %copy-start.2 = (s32[16]{0:T(128)S(1)}, s32[16]{0:T(128)}, u32[]{:S(2)}) copy-start(s32[16]{0:T(128)} %order_ref.1) | copy-start | bytes 196
  10.4 0.7 %copy-start.3 = (s32[64]{0:T(128)S(1)}, s32[64]{0:T(128)}, u32[]{:S(2)}) copy-start(s32[64]{0:T(128)} %cycle_ref.1) | copy-start | bytes 772
  10.4 0.7 %copy-start.4 = (s32[64]{0:T(128)S(1)}, s32[64]{0:T(128)}, u32[]{:S(2)}) copy-start(s32[64]{0:T(128)} %count_ref.1) | copy-start | bytes 772
  11.1 2.1 %copy-start.5 = (bf16[1,2560,64]{1,2,0:T(8,128)(2,1)S(1)}, bf16[1,2560,64]{1,2,0:T(8,128)(2,1)}, u32[]{:S(2)}) copy-start(bf16[1,2560,64]{1,2,0:T(8,128)(2,1)} %param.9) | copy-start | bytes 983044
  13.1 1.3 %collective-permute-start = (bf16[64,384]{1,0:T(8,128)(2,1)S(1)}, bf16[64,384]{1,0:T(8,128)(2,1)S(1)}, u32[]{:S(2)}, u32[]{:S(2)}) collective-permute-start(bf16[64,384]{1,0:T(8,128)(2,1)S(1)} %get-tuple-element.11), channel_id=1, source_target_pairs={{0,1},{1,0},{2,3},{3,2},{4,5},{5,4},{6,7},{7,6},{8,9},{9,8},{10,11... | collective-permute-start | bytes 147464 | tf_op jit(solution)/shard_map/ppermute | solution.py:308

commit v5 on v4

--- a/solution.py
+++ b/solution.py
@@ -17,9 +17,11 @@
 
 
 def member_order(blks):
-    quarter = blks // 4
+    pairs = blks // 2
+    quarter = pairs // 4
     order = [q * quarter + i for q in (2, 3, 1, 0) for i in reversed(range(quarter))]
-    return [k for k in order if k % 2 == 1] + [k for k in order if k % 2 == 0]
+    upper = [int(p >= pairs // 2) for p in range(pairs)]
+    return [2 * p + upper[p] for p in order] + [2 * p + 1 - upper[p] for p in order]
 
 
 def synth_kernel(blks, amps_hbm, beam_hbm, leg_hbm, out_ref, amps, beam, leg, weighted, sems):
@@ -135,7 +137,8 @@
     top = gram.astype(jnp.bfloat16)
     rest = (gram - top.astype(jnp.float32)).astype(jnp.bfloat16)
     whole[...] = jnp.concatenate([top, top, rest], axis=1)
-    mine = pl.multiple_of((1 - blk % 2) * rows, 16)
+    upper = (blk // 2 >= blks // 4).astype(jnp.int32)
+    mine = pl.multiple_of((blk + upper) % 2 * rows, 16)
     keep_ref[...] = whole[pl.ds(mine, rows), :]
     give_ref[...] = whole[pl.ds(pl.multiple_of(rows - mine, 16), rows), :]
 

time: 25.7 us -> 24.8 us (0.965)
  blocking collectives: 9.48 us -> 8.62 us
    all_to_all x1, blocking collectives: 9.48 us -> 8.62 us  [shards(): lax.all_to_all(half, ('band', 'blk'), split_axis=0, concat_axis=0, tiled=...]
where the time goes in v5:
time: 24.8 us; the launch traced here: 24.5 us
  blocking collectives  8.62 us (35%)
  starting transfers between devices  8.14 us (33%)
  Pallas kernels  6.14 us (25%)
  waiting for transfers between devices  0.87 us (4%)
  local copies, waits for them, and re-layouts  0.67 us (3%)
    all_to_all x1, blocking collectives, shards(): lax.all_to_all(half, ('band', 'blk'), split_axis=0, concat_axis=0, tiled=...  8.62 us
    all_to_all x1, starting transfers between devices, shards(): lax.all_to_all(sent, 'blk', split_axis=0, concat_axis=0, tiled=True, axis...  7.91 us
    pallas_call x1, Pallas kernels, shards(): pl.pallas_call(functools.partial(synth_kernel, blks), out_shape=jax.Shape...  2.41 us
    pallas_call x1, Pallas kernels, shards(): pl.pallas_call(functools.partial(gram_kernel, blks, bands), out_shape=[ja...  2 us
    pallas_call x1, Pallas kernels, shards(): pl.pallas_call(functools.partial(analysis_kernel, bands), out_shape=jax.S...  1.25 us
    ppermute x1, waiting for transfers between devices, shards(): got = lax.ppermute(give, 'blk', [(k, k ^ 1) for k in range(blks)])  0.87 us
    unnamed x12, local copies, waits for them, and re-layouts  0.66 us
  transfers between devices with their start and end apart: 2, of which 1 were waited for; matrix products, arithmetic and copies ran while one was open for 0% of the time, Pallas kernels for 9%

profile of v5, /device:TPU:0, one launch (start us, length us, event | category | flops | bytes accessed | tf_op | source)
XLA Modules:
  0.0 24.5 jit_solution(13112337950590576426)
XLA Ops:
  0.0 2.4 %shard_map.74 = f32[128,128]{1,0:T(8,128)} custom-call(bf16[2560,128]{1,0:T(8,128)(2,1)} %bitcast.21, f32[1,2560]{1,0:T(1,128)} %beam_hbm.1, bf16[64,2560]{1,0:T(8,128)(2,1)} %bitcast.20), custom_call_target="tpu_custom_call" | custom-call | flops 41943040 | bytes 983040 | tf_op jit(solution)/shard_map/pallas_call | solution.py:270
  2.4 0.0 copy-start
  2.4 0.0 copy-start.1
  2.4 7.9 %all-to-all-start = ((f32[16,8,128]{2,1,0:T(8,128)}), f32[16,8,128]{2,1,0:T(8,128)S(1)}, u32[]{:S(2)}, u32[]{:S(2)}) async-start(f32[16,8,128]{2,1,0:T(8,128)} %bitcast.22), calls=%async_computation | async-start | bytes 131072 | tf_op jit(solution)/shard_map/all_to_all | solution.py:287
  10.3 0.0 copy-start.2
  10.4 0.0 copy-start.3
  10.4 0.0 copy-start.4
  10.4 0.0 copy-done
  10.4 0.0 copy-done.1
  10.4 0.6 %copy-done.2 = s32[16]{0:T(128)S(1)} copy-done((s32[16]{0:T(128)S(1)}, s32[16]{0:T(128)}, u32[]{:S(2)}) %copy-start.2) | copy-done | bytes 88
  11.0 0.0 copy-done.3
  11.0 0.0 copy-done.4
  11.0 0.0 copy-start.5
  11.0 2.0 %shard_map.73 = (bf16[64,384]{1,0:T(8,128)(2,1)S(1)}, bf16[64,384]{1,0:T(8,128)(2,1)S(1)}, f32[16,128]{1,0:T(8,128)S(1)}) custom-call(s32[16]{0:T(128)S(1)} %copy-done.2, s32[64]{0:T(128)S(1)} %copy-done.3, s32[64]{0:T(128)S(1)} %copy-done.4, f32[4,4096]{1,0:T(4,128)S(1)} %bitcast.19, f32[1,2560]{1,0:T(1,128)S(1)} %copy-done), custom_call_target="tpu_custom_call" | custom-call | flops 268435456 | bytes 2097152 | tf_op jit(solution)/shard_map/pallas_call | solution.py:292
  13.0 0.2 collective-permute-start
  13.3 0.0 copy-done.5
  13.3 0.2 shard_map.76.leg_ref
  13.5 0.9 %collective-permute-done.got_ref = bf16[64,384]{1,0:T(8,128)(2,1)S(1)} collective-permute-done((bf16[64,384]{1,0:T(8,128)(2,1)S(1)}, bf16[64,384]{1,0:T(8,128)(2,1)S(1)}, u32[]{:S(2)}, u32[]{:S(2)}) %collective-permute-start) | collective-permute-done | bytes 49184 | tf_op jit(solution)/shard_map/ppermute | solution.py:311
  14.3 0.0 all-to-all-done
  14.3 0.3 %shard_map.75 = bf16[256,128]{1,0:T(8,128)(2,1)S(1)} custom-call(bf16[64,384]{1,0:T(8,128)(2,1)S(1)} %get-tuple-element.10.keep_ref, bf16[64,384]{1,0:T(8,128)(2,1)S(1)} %collective-permute-done.got_ref, f32[128,128]{1,0:T(8,128)S(1)} %bitcast.17, f32[16,128]{1,0:T(8,128)S(1)} %get-tuple-element.12.extra_ref), custom_call_target="tpu_custom_call" | custom-call | tf_op jit(solution)/shard_map/pallas_call | solution.py:323
  14.7 8.6 %all_to_all.22 = bf16[16,16,128]{2,1,0:T(8,128)(2,1)S(1)} all-to-all(bf16[16,16,128]{2,1,0:T(8,128)(2,1)S(1)} %bitcast.18), channel_id=1, replica_groups={{27,11,25,9,31,15,29,13,22,6,20,4,18,2,16,0},{26,10,24,8,30,14,28,12,23..., dimensions={0} | all-to-all | bytes 131072 | tf_op jit(solution)/shard_map/all_to_all | solution.py:336
  23.3 1.2 %shard_map.77 = f32[1280,128]{1,0:T(8,128)} custom-call(bf16[1280,64]{1,0:T(8,128)(2,1)S(1)} %shard_map.76.leg_ref, bf16[256,128]{1,0:T(8,128)(2,1)S(1)} %bitcast.16), custom_call_target="tpu_custom_call" | custom-call | tf_op jit(solution)/shard_map/pallas_call | solution.py:340
  (1 shorter events, 0.0 us)
Async XLA Ops:
  2.4 8.0 %copy-start = (f32[1,2560]{1,0:T(1,128)S(1)}, f32[1,2560]{1,0:T(1,128)}, u32[]{:S(2)}) copy-start(f32[1,2560]{1,0:T(1,128)} %beam_hbm.1) | copy-start | bytes 30724
  2.4 8.0 %copy-start.1 = (f32[1,4,4096]{2,1,0:T(4,128)S(1)}, f32[1,4,4096]{2,1,0:T(4,128)}, u32[]{:S(2)}) copy-start(f32[1,4,4096]{2,1,0:T(4,128)} %param.13) | copy-start | bytes 196612
  2.4 11.9 %all-to-all-start = ((f32[16,8,128]{2,1,0:T(8,128)}), f32[16,8,128]{2,1,0:T(8,128)S(1)}, u32[]{:S(2)}, u32[]{:S(2)}) async-start(f32[16,8,128]{2,1,0:T(8,128)} %bitcast.22), calls=%async_computation | async-start | bytes 131072 | tf_op jit(solution)/shard_map/all_to_all | solution.py:287
  10.3 0.7 %copy-start.2 = (s32[16]{0:T(128)S(1)}, s32[16]{0:T(128)}, u32[]{:S(2)}) copy-start(s32[16]{0:T(128)} %order_ref.1) | copy-start | bytes 196
  10.4 0.7 %copy-start.3 = (s32[64]{0:T(128)S(1)}, s32[64]{0:T(128)}, u32[]{:S(2)}) copy-start(s32[64]{0:T(128)} %cycle_ref.1) | copy-start | bytes 772
  10.4 0.7 %copy-start.4 = (s32[64]{0:T(128)S(1)}, s32[64]{0:T(128)}, u32[]{:S(2)}) copy-start(s32[64]{0:T(128)} %count_ref.1) | copy-start | bytes 772
  11.0 2.2 %copy-start.5 = (bf16[1,2560,64]{1,2,0:T(8,128)(2,1)S(1)}, bf16[1,2560,64]{1,2,0:T(8,128)(2,1)}, u32[]{:S(2)}) copy-start(bf16[1,2560,64]{1,2,0:T(8,128)(2,1)} %param.9) | copy-start | bytes 983044
  13.0 1.3 %collective-permute-start = (bf16[64,384]{1,0:T(8,128)(2,1)S(1)}, bf16[64,384]{1,0:T(8,128)(2,1)S(1)}, u32[]{:S(2)}, u32[]{:S(2)}) collective-permute-start(bf16[64,384]{1,0:T(8,128)(2,1)S(1)} %get-tuple-element.11), channel_id=1, source_target_pairs={{0,1},{1,0},{2,3},{3,2},{4,5},{5,4},{6,7},{7,6},{8,9},{9,8},{10,11... | collective-permute-start | bytes 147464 | tf_op jit(solution)/shard_map/ppermute | solution.py:311

commit v6 on v5

--- a/solution.py
+++ b/solution.py
@@ -24,22 +24,35 @@
     return [2 * p + upper[p] for p in order] + [2 * p + 1 - upper[p] for p in order]
 
 
-def synth_kernel(blks, amps_hbm, beam_hbm, leg_hbm, out_ref, amps, beam, leg, weighted, sems):
+def synth_kernel(
+    blks, bands, amps_hbm, beam_hbm, leg_hbm, order_hbm, cycle_hbm, count_hbm, noise_hbm,
+    out_ref, tables_ref, root_ref, extra_ref,
+    amps, beam, leg, weighted, order, cycle, count, noise, lists, sems,
+):
     degrees = amps.shape[0]
-    chunks = amps_hbm.shape[0] // SLAB
-    copies = [pltpu.make_async_copy(beam_hbm, beam, sems.at[0])]
+    cycles, pixels = noise.shape
+    chunks = degrees // SLAB
+    pairs = [(order_hbm, order), (cycle_hbm, cycle), (count_hbm, count), (beam_hbm, beam), (noise_hbm, noise)]
     for k in range(chunks):
         at = pl.ds(k * SLAB, SLAB)
-        copies.append(pltpu.make_async_copy(amps_hbm.at[at, :], amps.at[at, :], sems.at[1 + 2 * k]))
-    copies.append(pltpu.make_async_copy(leg_hbm, leg, sems.at[2]))
+        pairs.append((amps_hbm.at[at, :], amps.at[at, :]))
+    pairs.append((leg_hbm, leg))
+    copies = [pltpu.make_async_copy(src, dst, sems.at[n]) for n, (src, dst) in enumerate(pairs)]
     for copy in copies:
         copy.start()
-    copies[0].wait()
+    for copy in copies[:5]:
+        copy.wait()
+    *tables, counts = phase_tables(blks, pixels, cycles, order, cycle, count)
+    tables_ref[...] = jnp.concatenate(tables, axis=0)
+    pixel = lax.broadcasted_iota(jnp.int32, noise.shape, 1)
+    root = jnp.sqrt(jnp.where(pixel < counts[:cycles, :1], noise[...], 0.0))
+    root_ref[...] = jnp.concatenate([root] * (root_ref.shape[0] // cycles), axis=0)
+    extra_ref[...] = beam_rows(blks, bands, beam, lists)
     gains = jnp.concatenate(
         [beam[0:1, k * LANES : (k + 1) * LANES] for k in range(degrees // LANES)], axis=0
     ).T
     for k in range(chunks):
-        copies[1 + k].wait()
+        copies[5 + k].wait()
         for j in range(k * SLAB, (k + 1) * SLAB, LANES):
             product = amps[j : j + LANES, :].astype(jnp.float32) * gains[:, j // LANES : j // LANES + 1]
             weighted[j : j + LANES, :] = product.astype(jnp.bfloat16)
@@ -77,12 +90,9 @@
     return cos_out, sin_out
 
 
-def gram_kernel(blks, bands, order_ref, cycle_ref, count_ref, noise_ref, beam_ref, keep_ref, give_ref, extra_ref, high, low, whole, lists):
-    cycles, pixels = noise_ref.shape
-    orders = order_ref.shape[0]
-    rows = orders * cycles
-    blk = lax.axis_index("blk")
-    start = blk * cycles
+def phase_tables(blks, pixels, cycles, order_ref, cycle_ref, count_ref):
+    rows = blks * cycles
+    start = lax.axis_index("blk") * cycles
     row = lax.broadcasted_iota(jnp.int32, (rows, LANES), 0)
     lane = lax.broadcasted_iota(jnp.int32, (rows, LANES), 1)
     slot = row % cycles
@@ -99,22 +109,40 @@
     coarse = 2 * LANES * order * (lane & (pixels // LANES - 1)) + order * parity
     coarse_c, coarse_s = cos_sin(mod_exact(coarse, 2 * count), count)
     norm = lax.rsqrt(count.astype(jnp.float32))
-    fine_c, fine_s = fine_c * norm, fine_s * norm
-    coarse_s = -coarse_s
-
-    pixel = lax.broadcasted_iota(jnp.int32, (cycles, pixels), 1)
-    inside = pixel < count[:cycles, :1]
-    root = jnp.sqrt(jnp.where(inside, noise_ref[...], 0.0))
-    reps = max(8 // cycles, 1)
-    root = jnp.concatenate([root] * reps, axis=0)
-    period = root.shape[0]
-
+    return fine_c * norm, fine_s * norm, coarse_c, -coarse_s, count
+
+
+def beam_rows(blks, bands, beam_ref, lists):
+    blk = lax.axis_index("blk")
+    part = beam_ref.shape[1] // bands
+    lines = -(-part // LANES)
+    lists[...] = jnp.zeros_like(lists)
+    for p in range(bands):
+        for t in range(lines):
+            size = min(LANES, part - t * LANES)
+            first = p * part + t * LANES
+            value = beam_ref[0:1, first : first + size]
+            for term in range(TERMS):
+                top = value.astype(jnp.bfloat16).astype(jnp.float32)
+                at = p * (blks // 2) * EXTRA + term * lines + t
+                lists[at : at + 1, :size] = top
+                value = value - top
+    starts = [pl.multiple_of((p * (blks // 2) + blk // 2) * EXTRA, EXTRA) for p in range(bands)]
+    return jnp.concatenate([lists[pl.ds(at, EXTRA), :] for at in starts], axis=0)
+
+
+def gram_kernel(tables_ref, root_ref, keep_ref, give_ref, high, low, whole):
+    blks, blk = lax.axis_size("blk"), lax.axis_index("blk")
+    rows = keep_ref.shape[0]
+    cycles = rows // blks
+    period, pixels = root_ref.shape
+    fine_c, fine_s, coarse_c, coarse_s = (tables_ref[k * rows : (k + 1) * rows, :] for k in range(4))
     step = 2
     total = jnp.zeros((2 * rows, 4 * rows), jnp.float32)
     for block in range(pixels // LANES // step):
         for j in range(block * step, (block + 1) * step):
             cols = slice(j * LANES, (j + 1) * LANES)
-            here = jnp.concatenate([root[:, cols]] * (rows // period), axis=0)
+            here = jnp.concatenate([root_ref[:, cols]] * (rows // period), axis=0)
             a_c, a_s = coarse_c[:, j : j + 1], coarse_s[:, j : j + 1]
             for c, value in enumerate((a_c * fine_c + a_s * fine_s, a_s * fine_c - a_c * fine_s)):
                 value = value * here
@@ -136,31 +164,16 @@
     gram = jnp.where(row % cycles == col % cycles, gram, 0.0)
     top = gram.astype(jnp.bfloat16)
     rest = (gram - top.astype(jnp.float32)).astype(jnp.bfloat16)
-    whole[...] = jnp.concatenate([top, top, rest], axis=1)
+    whole[...] = jnp.concatenate([top, rest], axis=1)
     upper = (blk // 2 >= blks // 4).astype(jnp.int32)
     mine = pl.multiple_of((blk + upper) % 2 * rows, 16)
     keep_ref[...] = whole[pl.ds(mine, rows), :]
     give_ref[...] = whole[pl.ds(pl.multiple_of(rows - mine, 16), rows), :]
 
-    part = beam_ref.shape[1] // bands
-    lines = -(-part // LANES)
-    lists[...] = jnp.zeros_like(lists)
-    for p in range(bands):
-        for t in range(lines):
-            size = min(LANES, part - t * LANES)
-            first = p * part + t * LANES
-            value = beam_ref[0:1, first : first + size]
-            for term in range(TERMS):
-                top = value.astype(jnp.bfloat16).astype(jnp.float32)
-                at = p * (blks // 2) * EXTRA + term * lines + t
-                lists[at : at + 1, :size] = top
-                value = value - top
-        at = pl.multiple_of((p * (blks // 2) + blk // 2) * EXTRA, EXTRA)
-        extra_ref[p * EXTRA : (p + 1) * EXTRA, :] = lists[pl.ds(at, EXTRA), :]
-
 
 def apply_kernel(bands, keep_ref, got_ref, modes_ref, extra_ref, out_ref):
     rows = keep_ref.shape[0]
+    terms = keep_ref.shape[1] // 2
     pair, width = EXTRA, modes_ref.shape[1]
     chains = width // 2
     first = lax.axis_index("blk") % 2 == 0
@@ -185,6 +198,7 @@
         top = stacked.astype(jnp.bfloat16)
         rest = (stacked - top.astype(jnp.float32)).astype(jnp.bfloat16)
         right = jnp.concatenate([top, rest, top], axis=0)
+        matrix = jnp.concatenate([matrix[:, :terms], matrix], axis=1)
         result = jnp.dot(matrix, right, preferred_element_type=jnp.float32)
         half = jnp.concatenate([result[: rows // 2], result[rows // 2 :]], axis=1)
         halves.append(half.reshape(rows // 2 // pair, pair, width))
@@ -259,7 +273,6 @@
     rows = orders * cycles_here
     part = degrees // bands
     leg = jnp.swapaxes(legendre[0], 0, 1)
-    smem = pl.BlockSpec(memory_space=pltpu.SMEM)
     vmem = pl.BlockSpec(memory_space=pltpu.VMEM)
 
     hbm = pl.BlockSpec(memory_space=pltpu.HBM)
@@ -267,47 +280,51 @@
     pair = 2 * cycles_here
     assert orders == blks and blks % 2 == 0 and pair == EXTRA and cycles == cycles_here * blks
     slabs = degrees // SLAB
-    sent = pl.pallas_call(
-        functools.partial(synth_kernel, blks),
-        out_shape=jax.ShapeDtypeStruct((blks * pair, width), jnp.float32),
-        in_specs=[hbm] * 3,
-        out_specs=vmem,
+    pixels = inv_noise.shape[2]
+    period = cycles_here * max(8 // cycles_here, 1)
+    sent, tables, root, extra = pl.pallas_call(
+        functools.partial(synth_kernel, blks, bands),
+        out_shape=[
+            jax.ShapeDtypeStruct((blks * pair, width), jnp.float32),
+            pltpu.VMEM((4 * rows, LANES), jnp.float32),
+            pltpu.VMEM((period, pixels), jnp.float32),
+            pltpu.VMEM((bands * EXTRA, LANES), jnp.float32),
+        ],
+        in_specs=[hbm] * 7,
+        out_specs=[vmem] * 4,
         scratch_shapes=[
             pltpu.VMEM((degrees, width), jnp.bfloat16),
             pltpu.VMEM((1, degrees), jnp.float32),
             pltpu.VMEM((cycles, degrees), jnp.bfloat16),
             pltpu.VMEM((degrees, width), jnp.bfloat16),
-            pltpu.SemaphoreType.DMA((1 + 2 * slabs,)),
+            pltpu.SMEM(m_values.shape, jnp.int32),
+            pltpu.SMEM(cycle_order.shape, jnp.int32),
+            pltpu.SMEM(pixel_counts.shape, jnp.int32),
+            pltpu.VMEM((cycles_here, pixels), jnp.float32),
+            pltpu.VMEM((bands * (blks // 2) * EXTRA, LANES), jnp.float32),
+            pltpu.SemaphoreType.DMA((6 + slabs,)),
         ],
-        compiler_params=pltpu.CompilerParams(vmem_limit_bytes=127 * 512 * 1024),
+        compiler_params=pltpu.CompilerParams(vmem_limit_bytes=62 * 1024 * 1024),
         cost_estimate=pl.CostEstimate(
-            flops=2 * degrees * cycles * width, transcendentals=0, bytes_accessed=2 * degrees * (cycles + width)
+            flops=2000 * degrees * cycles * width, transcendentals=0, bytes_accessed=0
         ),
-    )(amps[:, 0, :], beam, leg)
+    )(amps[:, 0, :], beam, leg, m_values, cycle_order, pixel_counts, inv_noise[0])
     modes = lax.all_to_all(
         sent, "blk", split_axis=0, concat_axis=0, tiled=True, axis_index_groups=[member_order(blks)]
     )
 
-    pixels = inv_noise.shape[2]
-    keep, give, extra = pl.pallas_call(
-        functools.partial(gram_kernel, blks, bands),
-        out_shape=[
-            jax.ShapeDtypeStruct((rows, 6 * rows), jnp.bfloat16),
-            jax.ShapeDtypeStruct((rows, 6 * rows), jnp.bfloat16),
-            jax.ShapeDtypeStruct((bands * EXTRA, LANES), jnp.float32),
-        ],
-        in_specs=[smem] * 3 + [vmem] * 2,
-        out_specs=[vmem] * 3,
+    keep, give = pl.pallas_call(
+        gram_kernel,
+        out_shape=[jax.ShapeDtypeStruct((rows, 4 * rows), jnp.bfloat16)] * 2,
+        in_specs=[vmem] * 2,
+        out_specs=[vmem] * 2,
         scratch_shapes=[pltpu.VMEM((2 * rows, pixels), jnp.bfloat16)] * 2
-        + [
-            pltpu.VMEM((2 * rows, 6 * rows), jnp.bfloat16),
-            pltpu.VMEM((bands * (blks // 2) * EXTRA, LANES), jnp.float32),
-        ],
+        + [pltpu.VMEM((2 * rows, 4 * rows), jnp.bfloat16)],
         compiler_params=VMEM,
         cost_estimate=pl.CostEstimate(
             flops=16 * rows * rows * pixels, transcendentals=0, bytes_accessed=8 * rows * pixels
         ),
-    )(m_values, cycle_order, pixel_counts, inv_noise[0], beam)
+    )(tables, root)
     got = lax.ppermute(give, "blk", [(k, k ^ 1) for k in range(blks)])
 
     leg_part = lax.dynamic_slice_in_dim(leg, lax.axis_index("band") * part, part, axis=1)

time: 24.8 us -> 24.5 us (0.988)
  waiting for transfers between devices: 0.87 us -> 2.03 us
  local copies, waits for them, and re-layouts: 0.67 us -> 0.02 us
  Pallas kernels: 6.14 us -> 5.57 us
    all_to_all x1, waiting for transfers between devices: 0.01 us -> 1.19 us  [shards(): lax.all_to_all(sent, 'blk', split_axis=0, concat_axis=0, tiled=True, axis...]
    unnamed x12 -> x2, local copies, waits for them, and re-layouts: 0.66 us -> 0.01 us
    pallas_call x2, Pallas kernels: 4.41 us -> 3.83 us  [the longest x1 2.58 us: shards(): pl.pallas_call(functools.partial(synth_kernel, blks, bands), out_shape=[j...]
  transfers between devices with their start and end apart: 2 -> 2, of which waited for: 1 -> 2; matrix products, arithmetic and copies ran while one was open for 0% -> 0% of each run, Pallas kernels for 9% -> 6%
where the time goes in v6:
time: 24.5 us; the launch traced here: 24.3 us
  blocking collectives  8.62 us (35%)
  starting transfers between devices  8.01 us (33%)
  Pallas kernels  5.57 us (23%)
  waiting for transfers between devices  2.03 us (8%)
    all_to_all x1, blocking collectives, shards(): lax.all_to_all(half, ('band', 'blk'), split_axis=0, concat_axis=0, tiled=...  8.62 us
    all_to_all x1, starting transfers between devices, shards(): lax.all_to_all(sent, 'blk', split_axis=0, concat_axis=0, tiled=True, axis...  7.77 us
    pallas_call x1, Pallas kernels, shards(): pl.pallas_call(functools.partial(synth_kernel, blks, bands), out_shape=[j...  2.58 us
    pallas_call x1, Pallas kernels, shards(): pl.pallas_call(functools.partial(analysis_kernel, bands), out_shape=jax.S...  1.25 us
    pallas_call x1, Pallas kernels, shards(): pl.pallas_call(gram_kernel, out_shape=[jax.ShapeDtypeStruct((rows, 4 * ro...  1.25 us
    all_to_all x1, waiting for transfers between devices, shards(): lax.all_to_all(sent, 'blk', split_axis=0, concat_axis=0, tiled=True, axis...  1.19 us
    ppermute x1, waiting for transfers between devices, shards(): got = lax.ppermute(give, 'blk', [(k, k ^ 1) for k in range(blks)])  0.84 us
  transfers between devices with their start and end apart: 2, of which 2 were waited for; matrix products, arithmetic and copies ran while one was open for 0% of the time, Pallas kernels for 6%

profile of v6, /device:TPU:0, one launch (start us, length us, event | category | flops | bytes accessed | tf_op | source)
XLA Modules:
  0.0 24.3 jit_solution(13758556992647214561)
XLA Ops:
  0.0 2.6 %shard_map.73 = (f32[128,128]{1,0:T(8,128)}, f32[256,128]{1,0:T(8,128)S(1)}, f32[8,4096]{1,0:T(8,128)S(1)}, f32[16,128]{1,0:T(8,128)S(1)}) custom-call(bf16[2560,128]{1,0:T(8,128)(2,1)} %bitcast.21, f32[1,2560]{1,0:T(1,128)} %beam_hbm.1, bf16[64,2560]{1,0:T(8,128)(2,1)} %bitcast.19, s32[16]{0:T(128)} %order_hbm.1, s32[64]{0:T(128)} %cycle_hbm.1, ...), custom_call_target="tpu_custom_call" | custom-call | flops 41943040000 | tf_op jit(solution)/shard_map/pallas_call | solution.py:285
  2.6 7.8 %all-to-all-start = ((f32[16,8,128]{2,1,0:T(8,128)}), f32[16,8,128]{2,1,0:T(8,128)S(1)}, u32[]{:S(2)}, u32[]{:S(2)}) async-start(f32[16,8,128]{2,1,0:T(8,128)} %bitcast.20), calls=%async_computation | async-start | bytes 131072 | tf_op jit(solution)/shard_map/all_to_all | solution.py:312
  10.4 0.0 copy-start
  10.4 1.2 %shard_map.74 = (bf16[64,256]{1,0:T(8,128)(2,1)S(1)}, bf16[64,256]{1,0:T(8,128)(2,1)S(1)}) custom-call(f32[256,128]{1,0:T(8,128)S(1)} %get-tuple-element.13.tables_ref, f32[8,4096]{1,0:T(8,128)S(1)} %get-tuple-element.14.root_ref), custom_call_target="tpu_custom_call" | custom-call | flops 268435456 | bytes 2097152 | tf_op jit(solution)/shard_map/pallas_call | solution.py:316
  11.6 0.2 collective-permute-start
  11.9 0.0 copy-done
  11.9 0.2 shard_map.76.leg_ref
  12.1 0.8 %collective-permute-done.got_ref = bf16[64,256]{1,0:T(8,128)(2,1)S(1)} collective-permute-done((bf16[64,256]{1,0:T(8,128)(2,1)S(1)}, bf16[64,256]{1,0:T(8,128)(2,1)S(1)}, u32[]{:S(2)}, u32[]{:S(2)}) %collective-permute-start) | collective-permute-done | bytes 32800 | tf_op jit(solution)/shard_map/ppermute | solution.py:328
  12.9 1.2 %all-to-all-done = f32[16,8,128]{2,1,0:T(8,128)S(1)} async-done(((f32[16,8,128]{2,1,0:T(8,128)}), f32[16,8,128]{2,1,0:T(8,128)S(1)}, u32[]{:S(2)}, u32[]{:S(2)}) %all-to-all-start) | async-done | bytes 65568 | tf_op jit(solution)/shard_map/all_to_all | solution.py:312
  14.1 0.3 %shard_map.75 = bf16[256,128]{1,0:T(8,128)(2,1)S(1)} custom-call(bf16[64,256]{1,0:T(8,128)(2,1)S(1)} %get-tuple-element.15.keep_ref, bf16[64,256]{1,0:T(8,128)(2,1)S(1)} %collective-permute-done.got_ref, f32[128,128]{1,0:T(8,128)S(1)} %bitcast.16, f32[16,128]{1,0:T(8,128)S(1)} %get-tuple-element.18.extra_ref), custom_call_target="tpu_custom_call" | custom-call | tf_op jit(solution)/shard_map/pallas_call | solution.py:340
  14.4 8.6 %all_to_all.22 = bf16[16,16,128]{2,1,0:T(8,128)(2,1)S(1)} all-to-all(bf16[16,16,128]{2,1,0:T(8,128)(2,1)S(1)} %bitcast.17), channel_id=1, replica_groups={{27,11,25,9,31,15,29,13,22,6,20,4,18,2,16,0},{26,10,24,8,30,14,28,12,23..., dimensions={0} | all-to-all | bytes 131072 | tf_op jit(solution)/shard_map/all_to_all | solution.py:353
  23.0 1.3 %shard_map.77 = f32[1280,128]{1,0:T(8,128)} custom-call(bf16[1280,64]{1,0:T(8,128)(2,1)S(1)} %shard_map.76.leg_ref, bf16[256,128]{1,0:T(8,128)(2,1)S(1)} %bitcast.18), custom_call_target="tpu_custom_call" | custom-call | tf_op jit(solution)/shard_map/pallas_call | solution.py:357
  (1 shorter events, 0.0 us)
Async XLA Ops:
  2.6 11.5 %all-to-all-start = ((f32[16,8,128]{2,1,0:T(8,128)}), f32[16,8,128]{2,1,0:T(8,128)S(1)}, u32[]{:S(2)}, u32[]{:S(2)}) async-start(f32[16,8,128]{2,1,0:T(8,128)} %bitcast.20), calls=%async_computation | async-start | bytes 131072 | tf_op jit(solution)/shard_map/all_to_all | solution.py:312
  10.4 1.5 %copy-start = (bf16[1,2560,64]{1,2,0:T(8,128)(2,1)S(1)}, bf16[1,2560,64]{1,2,0:T(8,128)(2,1)}, u32[]{:S(2)}) copy-start(bf16[1,2560,64]{1,2,0:T(8,128)(2,1)} %param.9) | copy-start | bytes 983044
  11.6 1.3 %collective-permute-start = (bf16[64,256]{1,0:T(8,128)(2,1)S(1)}, bf16[64,256]{1,0:T(8,128)(2,1)S(1)}, u32[]{:S(2)}, u32[]{:S(2)}) collective-permute-start(bf16[64,256]{1,0:T(8,128)(2,1)S(1)} %get-tuple-element.16), channel_id=1, source_target_pairs={{0,1},{1,0},{2,3},{3,2},{4,5},{5,4},{6,7},{7,6},{8,9},{9,8},{10,11... | collective-permute-start | bytes 98312 | tf_op jit(solution)/shard_map/ppermute | solution.py:328

commit v7 on v6

--- a/solution.py
+++ b/solution.py
@@ -9,7 +9,7 @@
 from jax.sharding import PartitionSpec as P
 
 LANES = 128
-SLAB = 1280
+SLAB = 2560
 EXTRA = 8
 TERMS = 3
 VMEM = pltpu.CompilerParams(vmem_limit_bytes=48 * 1024 * 1024)
@@ -24,13 +24,28 @@
     return [2 * p + upper[p] for p in order] + [2 * p + 1 - upper[p] for p in order]
 
 
+def spread(rows, lines):
+    count = rows.shape[0]
+    term = lax.broadcasted_iota(jnp.int32, (count, lines * LANES), 0) % lines
+    block = lax.broadcasted_iota(jnp.int32, (count, lines * LANES), 1) // LANES
+    pick = jnp.where(term == block, 1.0, 0.0).astype(jnp.bfloat16)
+    return jnp.dot(rows.T.astype(jnp.bfloat16), pick, preferred_element_type=jnp.float32)
+
+
+def bf16_terms(value):
+    terms = []
+    for _ in range(TERMS):
+        terms.append(value.astype(jnp.bfloat16).astype(jnp.float32))
+        value = value - terms[-1]
+    return jnp.concatenate(terms, axis=0)
+
+
 def synth_kernel(
     blks, bands, amps_hbm, beam_hbm, leg_hbm, order_hbm, cycle_hbm, count_hbm, noise_hbm,
-    out_ref, tables_ref, root_ref, extra_ref,
-    amps, beam, leg, weighted, order, cycle, count, noise, lists, sems,
+    out_ref, order, cycle, count, noise, extra_ref,
+    amps, beam, leg, weighted, wide, lists, sems,
 ):
     degrees = amps.shape[0]
-    cycles, pixels = noise.shape
     chunks = degrees // SLAB
     pairs = [(order_hbm, order), (cycle_hbm, cycle), (count_hbm, count), (beam_hbm, beam), (noise_hbm, noise)]
     for k in range(chunks):
@@ -40,23 +55,18 @@
     copies = [pltpu.make_async_copy(src, dst, sems.at[n]) for n, (src, dst) in enumerate(pairs)]
     for copy in copies:
         copy.start()
-    for copy in copies[:5]:
-        copy.wait()
-    *tables, counts = phase_tables(blks, pixels, cycles, order, cycle, count)
-    tables_ref[...] = jnp.concatenate(tables, axis=0)
-    pixel = lax.broadcasted_iota(jnp.int32, noise.shape, 1)
-    root = jnp.sqrt(jnp.where(pixel < counts[:cycles, :1], noise[...], 0.0))
-    root_ref[...] = jnp.concatenate([root] * (root_ref.shape[0] // cycles), axis=0)
+    copies[3].wait()
+    lines = degrees // LANES
+    rows = jnp.concatenate([beam[0:1, k * LANES : (k + 1) * LANES] for k in range(lines)], axis=0)
+    wide[...] = spread(bf16_terms(rows), lines)
     extra_ref[...] = beam_rows(blks, bands, beam, lists)
-    gains = jnp.concatenate(
-        [beam[0:1, k * LANES : (k + 1) * LANES] for k in range(degrees // LANES)], axis=0
-    ).T
     for k in range(chunks):
         copies[5 + k].wait()
         for j in range(k * SLAB, (k + 1) * SLAB, LANES):
-            product = amps[j : j + LANES, :].astype(jnp.float32) * gains[:, j // LANES : j // LANES + 1]
+            product = amps[j : j + LANES, :].astype(jnp.float32) * wide[:, j : j + LANES]
             weighted[j : j + LANES, :] = product.astype(jnp.bfloat16)
-    copies[-1].wait()
+    for n in (0, 1, 2, 4, -1):
+        copies[n].wait()
     total = jnp.dot(leg[...], weighted[...], preferred_element_type=jnp.float32)
     pair = 2 * total.shape[0] // blks
     for g, k in enumerate(member_order(blks)):
@@ -131,18 +141,22 @@
     return jnp.concatenate([lists[pl.ds(at, EXTRA), :] for at in starts], axis=0)
 
 
-def gram_kernel(tables_ref, root_ref, keep_ref, give_ref, high, low, whole):
+def gram_kernel(order_ref, cycle_ref, count_ref, noise_ref, keep_ref, give_ref, high, low, whole):
     blks, blk = lax.axis_size("blk"), lax.axis_index("blk")
     rows = keep_ref.shape[0]
     cycles = rows // blks
-    period, pixels = root_ref.shape
-    fine_c, fine_s, coarse_c, coarse_s = (tables_ref[k * rows : (k + 1) * rows, :] for k in range(4))
+    pixels = noise_ref.shape[1]
+    fine_c, fine_s, coarse_c, coarse_s, count = phase_tables(blks, pixels, cycles, order_ref, cycle_ref, count_ref)
+    pixel = lax.broadcasted_iota(jnp.int32, noise_ref.shape, 1)
+    root = jnp.sqrt(jnp.where(pixel < count[:cycles, :1], noise_ref[...], 0.0))
+    root = jnp.concatenate([root] * max(8 // cycles, 1), axis=0)
+    period = root.shape[0]
     step = 2
     total = jnp.zeros((2 * rows, 4 * rows), jnp.float32)
     for block in range(pixels // LANES // step):
         for j in range(block * step, (block + 1) * step):
             cols = slice(j * LANES, (j + 1) * LANES)
-            here = jnp.concatenate([root_ref[:, cols]] * (rows // period), axis=0)
+            here = jnp.concatenate([root[:, cols]] * (rows // period), axis=0)
             a_c, a_s = coarse_c[:, j : j + 1], coarse_s[:, j : j + 1]
             for c, value in enumerate((a_c * fine_c + a_s * fine_s, a_s * fine_c - a_c * fine_s)):
                 value = value * here
@@ -273,6 +287,7 @@
     rows = orders * cycles_here
     part = degrees // bands
     leg = jnp.swapaxes(legendre[0], 0, 1)
+    smem = pl.BlockSpec(memory_space=pltpu.SMEM)
     vmem = pl.BlockSpec(memory_space=pltpu.VMEM)
 
     hbm = pl.BlockSpec(memory_space=pltpu.HBM)
@@ -281,26 +296,24 @@
     assert orders == blks and blks % 2 == 0 and pair == EXTRA and cycles == cycles_here * blks
     slabs = degrees // SLAB
     pixels = inv_noise.shape[2]
-    period = cycles_here * max(8 // cycles_here, 1)
-    sent, tables, root, extra = pl.pallas_call(
+    sent, *gram_inputs, extra = pl.pallas_call(
         functools.partial(synth_kernel, blks, bands),
         out_shape=[
             jax.ShapeDtypeStruct((blks * pair, width), jnp.float32),
-            pltpu.VMEM((4 * rows, LANES), jnp.float32),
-            pltpu.VMEM((period, pixels), jnp.float32),
+            pltpu.VMEM(m_values.shape, jnp.int32),
+            pltpu.VMEM(cycle_order.shape, jnp.int32),
+            pltpu.VMEM(pixel_counts.shape, jnp.int32),
+            pltpu.VMEM((cycles_here, pixels), jnp.float32),
             pltpu.VMEM((bands * EXTRA, LANES), jnp.float32),
         ],
         in_specs=[hbm] * 7,
-        out_specs=[vmem] * 4,
+        out_specs=[vmem] * 6,
         scratch_shapes=[
             pltpu.VMEM((degrees, width), jnp.bfloat16),
             pltpu.VMEM((1, degrees), jnp.float32),
             pltpu.VMEM((cycles, degrees), jnp.bfloat16),
             pltpu.VMEM((degrees, width), jnp.bfloat16),
-            pltpu.SMEM(m_values.shape, jnp.int32),
-            pltpu.SMEM(cycle_order.shape, jnp.int32),
-            pltpu.SMEM(pixel_counts.shape, jnp.int32),
-            pltpu.VMEM((cycles_here, pixels), jnp.float32),
+            pltpu.VMEM((LANES, degrees), jnp.float32),
             pltpu.VMEM((bands * (blks // 2) * EXTRA, LANES), jnp.float32),
             pltpu.SemaphoreType.DMA((6 + slabs,)),
         ],
@@ -316,7 +329,7 @@
     keep, give = pl.pallas_call(
         gram_kernel,
         out_shape=[jax.ShapeDtypeStruct((rows, 4 * rows), jnp.bfloat16)] * 2,
-        in_specs=[vmem] * 2,
+        in_specs=[smem] * 3 + [vmem],
         out_specs=[vmem] * 2,
         scratch_shapes=[pltpu.VMEM((2 * rows, pixels), jnp.bfloat16)] * 2
         + [pltpu.VMEM((2 * rows, 4 * rows), jnp.bfloat16)],
@@ -324,7 +337,7 @@
         cost_estimate=pl.CostEstimate(
             flops=16 * rows * rows * pixels, transcendentals=0, bytes_accessed=8 * rows * pixels
         ),
-    )(tables, root)
+    )(*gram_inputs)
     got = lax.ppermute(give, "blk", [(k, k ^ 1) for k in range(blks)])
 
     leg_part = lax.dynamic_slice_in_dim(leg, lax.axis_index("band") * part, part, axis=1)

time: 24.5 us -> 24.2 us (0.988)
  waiting for transfers between devices: 2.03 us -> 1.29 us
  Pallas kernels: 5.57 us -> 5.95 us
    all_to_all x1, waiting for transfers between devices: 1.19 us -> 0.45 us  [shards(): lax.all_to_all(sent, 'blk', split_axis=0, concat_axis=0, tiled=True, axis...]
    pallas_call x1, Pallas kernels: 1.25 us -> 1.99 us  [shards(): pl.pallas_call(gram_kernel, out_shape=[jax.ShapeDtypeStruct((rows, 4 * ro...]
    pallas_call x1, Pallas kernels: 2.58 us -> 2.23 us  [shards(): pl.pallas_call(functools.partial(synth_kernel, blks, bands), out_shape=[j...]
  transfers between devices with their start and end apart: 2 -> 2, of which waited for: 2 -> 2; matrix products, arithmetic and copies ran while one was open for 0% -> 0% of each run, Pallas kernels for 6% -> 9%
where the time goes in v7:
time: 24.2 us; the launch traced here: 23.9 us
  blocking collectives  8.62 us (36%)
  starting transfers between devices  8.01 us (33%)
  Pallas kernels  5.95 us (25%)
  waiting for transfers between devices  1.29 us (5%)
    all_to_all x1, blocking collectives, shards(): lax.all_to_all(half, ('band', 'blk'), split_axis=0, concat_axis=0, tiled=...  8.62 us
    all_to_all x1, starting transfers between devices, shards(): lax.all_to_all(sent, 'blk', split_axis=0, concat_axis=0, tiled=True, axis...  7.78 us
    pallas_call x1, Pallas kernels, shards(): pl.pallas_call(functools.partial(synth_kernel, blks, bands), out_shape=[j...  2.23 us
    pallas_call x1, Pallas kernels, shards(): pl.pallas_call(gram_kernel, out_shape=[jax.ShapeDtypeStruct((rows, 4 * ro...  1.99 us
    pallas_call x1, Pallas kernels, shards(): pl.pallas_call(functools.partial(analysis_kernel, bands), out_shape=jax.S...  1.25 us
    ppermute x1, waiting for transfers between devices, shards(): got = lax.ppermute(give, 'blk', [(k, k ^ 1) for k in range(blks)])  0.84 us
  transfers between devices with their start and end apart: 2, of which 2 were waited for; matrix products, arithmetic and copies ran while one was open for 0% of the time, Pallas kernels for 9%

profile of v7, /device:TPU:0, one launch (start us, length us, event | category | flops | bytes accessed | tf_op | source)
XLA Modules:
  0.0 23.9 jit_solution(8813701602523360481)
XLA Ops:
  0.0 2.2 %shard_map.73 = (f32[128,128]{1,0:T(8,128)}, s32[16]{0:T(128)S(1)}, s32[64]{0:T(128)S(1)}, s32[64]{0:T(128)S(1)}, f32[4,4096]{1,0:T(4,128)S(1)}, /*index=5*/f32[16,128]{1,0:T(8,128)S(1)}) custom-call(bf16[2560,128]{1,0:T(8,128)(2,1)} %bitcast.21, f32[1,2560]{1,0:T(1,128)} %beam_hbm.1, bf16[64,2560]{1,0:T(8,128)(2,1)} %bitcast.19, s32[16]{0:T(128)} %order_hbm.1, ...), custom_call_target="tpu_custom_call" | custom-call | flops 41943040000 | tf_op jit(solution)/shard_map/pallas_call | solution.py:299
  2.2 7.8 %all-to-all-start = ((f32[16,8,128]{2,1,0:T(8,128)}), f32[16,8,128]{2,1,0:T(8,128)S(1)}, u32[]{:S(2)}, u32[]{:S(2)}) async-start(f32[16,8,128]{2,1,0:T(8,128)} %bitcast.20), calls=%async_computation | async-start | bytes 131072 | tf_op jit(solution)/shard_map/all_to_all | solution.py:325
  10.0 0.0 copy-start
  10.0 2.0 %shard_map.74 = (bf16[64,256]{1,0:T(8,128)(2,1)S(1)}, bf16[64,256]{1,0:T(8,128)(2,1)S(1)}) custom-call(s32[16]{0:T(128)S(1)} %get-tuple-element.15.order_ref, s32[64]{0:T(128)S(1)} %get-tuple-element.16.cycle_ref, s32[64]{0:T(128)S(1)} %get-tuple-element.17.count_ref, f32[4,4096]{1,0:T(4,128)S(1)} %get-tuple-element.18.noise_ref), custom_call_target="tpu_custom_call" | custom-call | flops 268435456 | bytes 2097152 | tf_op jit(solution)/shard_map/pallas_call | solution.py:329
  12.0 0.2 collective-permute-start
  12.3 0.0 copy-done
  12.3 0.2 shard_map.76.leg_ref
  12.4 0.8 %collective-permute-done.got_ref = bf16[64,256]{1,0:T(8,128)(2,1)S(1)} collective-permute-done((bf16[64,256]{1,0:T(8,128)(2,1)S(1)}, bf16[64,256]{1,0:T(8,128)(2,1)S(1)}, u32[]{:S(2)}, u32[]{:S(2)}) %collective-permute-start) | collective-permute-done | bytes 32800 | tf_op jit(solution)/shard_map/ppermute | solution.py:341
  13.3 0.5 %all-to-all-done = f32[16,8,128]{2,1,0:T(8,128)S(1)} async-done(((f32[16,8,128]{2,1,0:T(8,128)}), f32[16,8,128]{2,1,0:T(8,128)S(1)}, u32[]{:S(2)}, u32[]{:S(2)}) %all-to-all-start) | async-done | bytes 65568 | tf_op jit(solution)/shard_map/all_to_all | solution.py:325
  13.7 0.3 %shard_map.75 = bf16[256,128]{1,0:T(8,128)(2,1)S(1)} custom-call(bf16[64,256]{1,0:T(8,128)(2,1)S(1)} %get-tuple-element.19.keep_ref, bf16[64,256]{1,0:T(8,128)(2,1)S(1)} %collective-permute-done.got_ref, f32[128,128]{1,0:T(8,128)S(1)} %bitcast.16, f32[16,128]{1,0:T(8,128)S(1)} %get-tuple-element.22.extra_ref), custom_call_target="tpu_custom_call" | custom-call | tf_op jit(solution)/shard_map/pallas_call | solution.py:353
  14.1 8.6 %all_to_all.22 = bf16[16,16,128]{2,1,0:T(8,128)(2,1)S(1)} all-to-all(bf16[16,16,128]{2,1,0:T(8,128)(2,1)S(1)} %bitcast.17), channel_id=1, replica_groups={{27,11,25,9,31,15,29,13,22,6,20,4,18,2,16,0},{26,10,24,8,30,14,28,12,23..., dimensions={0} | all-to-all | bytes 131072 | tf_op jit(solution)/shard_map/all_to_all | solution.py:366
  22.7 1.2 %shard_map.77 = f32[1280,128]{1,0:T(8,128)} custom-call(bf16[1280,64]{1,0:T(8,128)(2,1)S(1)} %shard_map.76.leg_ref, bf16[256,128]{1,0:T(8,128)(2,1)S(1)} %bitcast.18), custom_call_target="tpu_custom_call" | custom-call | tf_op jit(solution)/shard_map/pallas_call | solution.py:370
  (1 shorter events, 0.0 us)
Async XLA Ops:
  2.2 11.5 %all-to-all-start = ((f32[16,8,128]{2,1,0:T(8,128)}), f32[16,8,128]{2,1,0:T(8,128)S(1)}, u32[]{:S(2)}, u32[]{:S(2)}) async-start(f32[16,8,128]{2,1,0:T(8,128)} %bitcast.20), calls=%async_computation | async-start | bytes 131072 | tf_op jit(solution)/shard_map/all_to_all | solution.py:325
  10.0 2.2 %copy-start = (bf16[1,2560,64]{1,2,0:T(8,128)(2,1)S(1)}, bf16[1,2560,64]{1,2,0:T(8,128)(2,1)}, u32[]{:S(2)}) copy-start(bf16[1,2560,64]{1,2,0:T(8,128)(2,1)} %param.9) | copy-start | bytes 983044
  12.0 1.3 %collective-permute-start = (bf16[64,256]{1,0:T(8,128)(2,1)S(1)}, bf16[64,256]{1,0:T(8,128)(2,1)S(1)}, u32[]{:S(2)}, u32[]{:S(2)}) collective-permute-start(bf16[64,256]{1,0:T(8,128)(2,1)S(1)} %get-tuple-element.20), channel_id=1, source_target_pairs={{0,1},{1,0},{2,3},{3,2},{4,5},{5,4},{6,7},{7,6},{8,9},{9,8},{10,11... | collective-permute-start | bytes 98312 | tf_op jit(solution)/shard_map/ppermute | solution.py:341

commit v8 on v7

--- a/solution.py
+++ b/solution.py
@@ -53,7 +53,7 @@
         pairs.append((amps_hbm.at[at, :], amps.at[at, :]))
     pairs.append((leg_hbm, leg))
     copies = [pltpu.make_async_copy(src, dst, sems.at[n]) for n, (src, dst) in enumerate(pairs)]
-    for copy in copies:
+    for copy in copies[3:4] + copies[5:] + copies[:3] + copies[4:5]:
         copy.start()
     copies[3].wait()
     lines = degrees // LANES

time: 24.2 us -> 24.2 us (level)
  no operation moved by 1% of the time
where the time goes in v8:
time: 24.2 us; the launch traced here: 23.8 us
  blocking collectives  8.63 us (36%)
  starting transfers between devices  8.01 us (33%)
  Pallas kernels  5.88 us (24%)
  waiting for transfers between devices  1.29 us (5%)
    all_to_all x1, blocking collectives, shards(): lax.all_to_all(half, ('band', 'blk'), split_axis=0, concat_axis=0, tiled=...  8.63 us
    all_to_all x1, starting transfers between devices, shards(): lax.all_to_all(sent, 'blk', split_axis=0, concat_axis=0, tiled=True, axis...  7.77 us
    pallas_call x1, Pallas kernels, shards(): pl.pallas_call(functools.partial(synth_kernel, blks, bands), out_shape=[j...  2.16 us
    pallas_call x1, Pallas kernels, shards(): pl.pallas_call(gram_kernel, out_shape=[jax.ShapeDtypeStruct((rows, 4 * ro...  1.99 us
    pallas_call x1, Pallas kernels, shards(): pl.pallas_call(functools.partial(analysis_kernel, bands), out_shape=jax.S...  1.25 us
    ppermute x1, waiting for transfers between devices, shards(): got = lax.ppermute(give, 'blk', [(k, k ^ 1) for k in range(blks)])  0.84 us
  transfers between devices with their start and end apart: 2, of which 2 were waited for; matrix products, arithmetic and copies ran while one was open for 0% of the time, Pallas kernels for 9%

profile of v8, /device:TPU:0, one launch (start us, length us, event | category | flops | bytes accessed | tf_op | source)
XLA Modules:
  0.0 23.8 jit_solution(11775786155949972817)
XLA Ops:
  0.0 2.2 %shard_map.73 = (f32[128,128]{1,0:T(8,128)}, s32[16]{0:T(128)S(1)}, s32[64]{0:T(128)S(1)}, s32[64]{0:T(128)S(1)}, f32[4,4096]{1,0:T(4,128)S(1)}, /*index=5*/f32[16,128]{1,0:T(8,128)S(1)}) custom-call(bf16[2560,128]{1,0:T(8,128)(2,1)} %bitcast.21, f32[1,2560]{1,0:T(1,128)} %beam_hbm.1, bf16[64,2560]{1,0:T(8,128)(2,1)} %bitcast.19, s32[16]{0:T(128)} %order_hbm.1, ...), custom_call_target="tpu_custom_call" | custom-call | flops 41943040000 | tf_op jit(solution)/shard_map/pallas_call | solution.py:299
  2.2 7.8 %all-to-all-start = ((f32[16,8,128]{2,1,0:T(8,128)}), f32[16,8,128]{2,1,0:T(8,128)S(1)}, u32[]{:S(2)}, u32[]{:S(2)}) async-start(f32[16,8,128]{2,1,0:T(8,128)} %bitcast.20), calls=%async_computation | async-start | bytes 131072 | tf_op jit(solution)/shard_map/all_to_all | solution.py:325
  9.9 0.0 copy-start
  9.9 2.0 %shard_map.74 = (bf16[64,256]{1,0:T(8,128)(2,1)S(1)}, bf16[64,256]{1,0:T(8,128)(2,1)S(1)}) custom-call(s32[16]{0:T(128)S(1)} %get-tuple-element.15.order_ref, s32[64]{0:T(128)S(1)} %get-tuple-element.16.cycle_ref, s32[64]{0:T(128)S(1)} %get-tuple-element.17.count_ref, f32[4,4096]{1,0:T(4,128)S(1)} %get-tuple-element.18.noise_ref), custom_call_target="tpu_custom_call" | custom-call | flops 268435456 | bytes 2097152 | tf_op jit(solution)/shard_map/pallas_call | solution.py:329
  11.9 0.2 collective-permute-start
  12.2 0.0 copy-done
  12.2 0.2 shard_map.76.leg_ref
  12.4 0.8 %collective-permute-done.got_ref = bf16[64,256]{1,0:T(8,128)(2,1)S(1)} collective-permute-done((bf16[64,256]{1,0:T(8,128)(2,1)S(1)}, bf16[64,256]{1,0:T(8,128)(2,1)S(1)}, u32[]{:S(2)}, u32[]{:S(2)}) %collective-permute-start) | collective-permute-done | bytes 32800 | tf_op jit(solution)/shard_map/ppermute | solution.py:341
  13.2 0.5 %all-to-all-done = f32[16,8,128]{2,1,0:T(8,128)S(1)} async-done(((f32[16,8,128]{2,1,0:T(8,128)}), f32[16,8,128]{2,1,0:T(8,128)S(1)}, u32[]{:S(2)}, u32[]{:S(2)}) %all-to-all-start) | async-done | bytes 65568 | tf_op jit(solution)/shard_map/all_to_all | solution.py:325
  13.7 0.3 %shard_map.75 = bf16[256,128]{1,0:T(8,128)(2,1)S(1)} custom-call(bf16[64,256]{1,0:T(8,128)(2,1)S(1)} %get-tuple-element.19.keep_ref, bf16[64,256]{1,0:T(8,128)(2,1)S(1)} %collective-permute-done.got_ref, f32[128,128]{1,0:T(8,128)S(1)} %bitcast.16, f32[16,128]{1,0:T(8,128)S(1)} %get-tuple-element.22.extra_ref), custom_call_target="tpu_custom_call" | custom-call | tf_op jit(solution)/shard_map/pallas_call | solution.py:353
  14.0 8.6 %all_to_all.22 = bf16[16,16,128]{2,1,0:T(8,128)(2,1)S(1)} all-to-all(bf16[16,16,128]{2,1,0:T(8,128)(2,1)S(1)} %bitcast.17), channel_id=1, replica_groups={{27,11,25,9,31,15,29,13,22,6,20,4,18,2,16,0},{26,10,24,8,30,14,28,12,23..., dimensions={0} | all-to-all | bytes 131072 | tf_op jit(solution)/shard_map/all_to_all | solution.py:366
  22.6 1.2 %shard_map.77 = f32[1280,128]{1,0:T(8,128)} custom-call(bf16[1280,64]{1,0:T(8,128)(2,1)S(1)} %shard_map.76.leg_ref, bf16[256,128]{1,0:T(8,128)(2,1)S(1)} %bitcast.18), custom_call_target="tpu_custom_call" | custom-call | tf_op jit(solution)/shard_map/pallas_call | solution.py:370
  (1 shorter events, 0.0 us)
Async XLA Ops:
  2.2 11.5 %all-to-all-start = ((f32[16,8,128]{2,1,0:T(8,128)}), f32[16,8,128]{2,1,0:T(8,128)S(1)}, u32[]{:S(2)}, u32[]{:S(2)}) async-start(f32[16,8,128]{2,1,0:T(8,128)} %bitcast.20), calls=%async_computation | async-start | bytes 131072 | tf_op jit(solution)/shard_map/all_to_all | solution.py:325
  9.9 2.2 %copy-start = (bf16[1,2560,64]{1,2,0:T(8,128)(2,1)S(1)}, bf16[1,2560,64]{1,2,0:T(8,128)(2,1)}, u32[]{:S(2)}) copy-start(bf16[1,2560,64]{1,2,0:T(8,128)(2,1)} %param.9) | copy-start | bytes 983044
  11.9 1.3 %collective-permute-start = (bf16[64,256]{1,0:T(8,128)(2,1)S(1)}, bf16[64,256]{1,0:T(8,128)(2,1)S(1)}, u32[]{:S(2)}, u32[]{:S(2)}) collective-permute-start(bf16[64,256]{1,0:T(8,128)(2,1)S(1)} %get-tuple-element.20), channel_id=1, source_target_pairs={{0,1},{1,0},{2,3},{3,2},{4,5},{5,4},{6,7},{7,6},{8,9},{9,8},{10,11... | collective-permute-start | bytes 98312 | tf_op jit(solution)/shard_map/ppermute | solution.py:341

commit v9 on v8

--- a/solution.py
+++ b/solution.py
@@ -9,7 +9,7 @@
 from jax.sharding import PartitionSpec as P
 
 LANES = 128
-SLAB = 2560
+SLAB = 1280
 EXTRA = 8
 TERMS = 3
 VMEM = pltpu.CompilerParams(vmem_limit_bytes=48 * 1024 * 1024)

time: 24.2 us -> 24.2 us (level)
  no operation moved by 1% of the time
where the time goes in v9:
time: 24.2 us; the launch traced here: 23.9 us
  blocking collectives  8.63 us (36%)
  starting transfers between devices  8 us (33%)
  Pallas kernels  5.9 us (24%)
  waiting for transfers between devices  1.29 us (5%)
    all_to_all x1, blocking collectives, shards(): lax.all_to_all(half, ('band', 'blk'), split_axis=0, concat_axis=0, tiled=...  8.63 us
    all_to_all x1, starting transfers between devices, shards(): lax.all_to_all(sent, 'blk', split_axis=0, concat_axis=0, tiled=True, axis...  7.77 us
    pallas_call x1, Pallas kernels, shards(): pl.pallas_call(functools.partial(synth_kernel, blks, bands), out_shape=[j...  2.17 us
    pallas_call x1, Pallas kernels, shards(): pl.pallas_call(gram_kernel, out_shape=[jax.ShapeDtypeStruct((rows, 4 * ro...  1.99 us
    pallas_call x1, Pallas kernels, shards(): pl.pallas_call(functools.partial(analysis_kernel, bands), out_shape=jax.S...  1.25 us
    ppermute x1, waiting for transfers between devices, shards(): got = lax.ppermute(give, 'blk', [(k, k ^ 1) for k in range(blks)])  0.85 us
  transfers between devices with their start and end apart: 2, of which 2 were waited for; matrix products, arithmetic and copies ran while one was open for 0% of the time, Pallas kernels for 9%

profile of v9, /device:TPU:0, one launch (start us, length us, event | category | flops | bytes accessed | tf_op | source)
XLA Modules:
  0.0 23.9 jit_solution(16234393349682959144)
XLA Ops:
  0.0 2.2 %shard_map.73 = (f32[128,128]{1,0:T(8,128)}, s32[16]{0:T(128)S(1)}, s32[64]{0:T(128)S(1)}, s32[64]{0:T(128)S(1)}, f32[4,4096]{1,0:T(4,128)S(1)}, /*index=5*/f32[16,128]{1,0:T(8,128)S(1)}) custom-call(bf16[2560,128]{1,0:T(8,128)(2,1)} %bitcast.21, f32[1,2560]{1,0:T(1,128)} %beam_hbm.1, bf16[64,2560]{1,0:T(8,128)(2,1)} %bitcast.19, s32[16]{0:T(128)} %order_hbm.1, ...), custom_call_target="tpu_custom_call" | custom-call | flops 41943040000 | tf_op jit(solution)/shard_map/pallas_call | solution.py:299
  2.2 7.8 %all-to-all-start = ((f32[16,8,128]{2,1,0:T(8,128)}), f32[16,8,128]{2,1,0:T(8,128)S(1)}, u32[]{:S(2)}, u32[]{:S(2)}) async-start(f32[16,8,128]{2,1,0:T(8,128)} %bitcast.20), calls=%async_computation | async-start | bytes 131072 | tf_op jit(solution)/shard_map/all_to_all | solution.py:325
  9.9 0.0 copy-start
  10.0 2.0 %shard_map.74 = (bf16[64,256]{1,0:T(8,128)(2,1)S(1)}, bf16[64,256]{1,0:T(8,128)(2,1)S(1)}) custom-call(s32[16]{0:T(128)S(1)} %get-tuple-element.15.order_ref, s32[64]{0:T(128)S(1)} %get-tuple-element.16.cycle_ref, s32[64]{0:T(128)S(1)} %get-tuple-element.17.count_ref, f32[4,4096]{1,0:T(4,128)S(1)} %get-tuple-element.18.noise_ref), custom_call_target="tpu_custom_call" | custom-call | flops 268435456 | bytes 2097152 | tf_op jit(solution)/shard_map/pallas_call | solution.py:329
  11.9 0.2 collective-permute-start
  12.2 0.0 copy-done
  12.2 0.2 shard_map.76.leg_ref
  12.4 0.8 %collective-permute-done.got_ref = bf16[64,256]{1,0:T(8,128)(2,1)S(1)} collective-permute-done((bf16[64,256]{1,0:T(8,128)(2,1)S(1)}, bf16[64,256]{1,0:T(8,128)(2,1)S(1)}, u32[]{:S(2)}, u32[]{:S(2)}) %collective-permute-start) | collective-permute-done | bytes 32800 | tf_op jit(solution)/shard_map/ppermute | solution.py:341
  13.2 0.4 %all-to-all-done = f32[16,8,128]{2,1,0:T(8,128)S(1)} async-done(((f32[16,8,128]{2,1,0:T(8,128)}), f32[16,8,128]{2,1,0:T(8,128)S(1)}, u32[]{:S(2)}, u32[]{:S(2)}) %all-to-all-start) | async-done | bytes 65568 | tf_op jit(solution)/shard_map/all_to_all | solution.py:325
  13.7 0.3 %shard_map.75 = bf16[256,128]{1,0:T(8,128)(2,1)S(1)} custom-call(bf16[64,256]{1,0:T(8,128)(2,1)S(1)} %get-tuple-element.19.keep_ref, bf16[64,256]{1,0:T(8,128)(2,1)S(1)} %collective-permute-done.got_ref, f32[128,128]{1,0:T(8,128)S(1)} %bitcast.16, f32[16,128]{1,0:T(8,128)S(1)} %get-tuple-element.22.extra_ref), custom_call_target="tpu_custom_call" | custom-call | tf_op jit(solution)/shard_map/pallas_call | solution.py:353
  14.0 8.6 %all_to_all.22 = bf16[16,16,128]{2,1,0:T(8,128)(2,1)S(1)} all-to-all(bf16[16,16,128]{2,1,0:T(8,128)(2,1)S(1)} %bitcast.17), channel_id=1, replica_groups={{27,11,25,9,31,15,29,13,22,6,20,4,18,2,16,0},{26,10,24,8,30,14,28,12,23..., dimensions={0} | all-to-all | bytes 131072 | tf_op jit(solution)/shard_map/all_to_all | solution.py:366
  22.6 1.3 %shard_map.77 = f32[1280,128]{1,0:T(8,128)} custom-call(bf16[1280,64]{1,0:T(8,128)(2,1)S(1)} %shard_map.76.leg_ref, bf16[256,128]{1,0:T(8,128)(2,1)S(1)} %bitcast.18), custom_call_target="tpu_custom_call" | custom-call | tf_op jit(solution)/shard_map/pallas_call | solution.py:370
  (1 shorter events, 0.0 us)
Async XLA Ops:
  2.2 11.5 %all-to-all-start = ((f32[16,8,128]{2,1,0:T(8,128)}), f32[16,8,128]{2,1,0:T(8,128)S(1)}, u32[]{:S(2)}, u32[]{:S(2)}) async-start(f32[16,8,128]{2,1,0:T(8,128)} %bitcast.20), calls=%async_computation | async-start | bytes 131072 | tf_op jit(solution)/shard_map/all_to_all | solution.py:325
  9.9 2.2 %copy-start = (bf16[1,2560,64]{1,2,0:T(8,128)(2,1)S(1)}, bf16[1,2560,64]{1,2,0:T(8,128)(2,1)}, u32[]{:S(2)}) copy-start(bf16[1,2560,64]{1,2,0:T(8,128)(2,1)} %param.9) | copy-start | bytes 983044
  11.9 1.3 %collective-permute-start = (bf16[64,256]{1,0:T(8,128)(2,1)S(1)}, bf16[64,256]{1,0:T(8,128)(2,1)S(1)}, u32[]{:S(2)}, u32[]{:S(2)}) collective-permute-start(bf16[64,256]{1,0:T(8,128)(2,1)S(1)} %get-tuple-element.20), channel_id=1, source_target_pairs={{0,1},{1,0},{2,3},{3,2},{4,5},{5,4},{6,7},{7,6},{8,9},{9,8},{10,11... | collective-permute-start | bytes 98312 | tf_op jit(solution)/shard_map/ppermute | solution.py:341

commit v10 on v9

--- a/solution.py
+++ b/solution.py
@@ -51,7 +51,9 @@
     for k in range(chunks):
         at = pl.ds(k * SLAB, SLAB)
         pairs.append((amps_hbm.at[at, :], amps.at[at, :]))
-    pairs.append((leg_hbm, leg))
+    half = leg.shape[0] // 2
+    for k in range(2):
+        pairs.append((leg_hbm.at[pl.ds(k * half, half), :], leg.at[pl.ds(k * half, half), :]))
     copies = [pltpu.make_async_copy(src, dst, sems.at[n]) for n, (src, dst) in enumerate(pairs)]
     for copy in copies[3:4] + copies[5:] + copies[:3] + copies[4:5]:
         copy.start()
@@ -65,7 +67,7 @@
         for j in range(k * SLAB, (k + 1) * SLAB, LANES):
             product = amps[j : j + LANES, :].astype(jnp.float32) * wide[:, j : j + LANES]
             weighted[j : j + LANES, :] = product.astype(jnp.bfloat16)
-    for n in (0, 1, 2, 4, -1):
+    for n in (0, 1, 2, 4, -2, -1):
         copies[n].wait()
     total = jnp.dot(leg[...], weighted[...], preferred_element_type=jnp.float32)
     pair = 2 * total.shape[0] // blks
@@ -315,7 +317,7 @@
             pltpu.VMEM((degrees, width), jnp.bfloat16),
             pltpu.VMEM((LANES, degrees), jnp.float32),
             pltpu.VMEM((bands * (blks // 2) * EXTRA, LANES), jnp.float32),
-            pltpu.SemaphoreType.DMA((6 + slabs,)),
+            pltpu.SemaphoreType.DMA((7 + slabs,)),
         ],
         compiler_params=pltpu.CompilerParams(vmem_limit_bytes=62 * 1024 * 1024),
         cost_estimate=pl.CostEstimate(

time: 24.2 us -> 24.2 us (level)
  no operation moved by 1% of the time
where the time goes in v10:
time: 24.2 us; the launch traced here: 23.9 us
  blocking collectives  8.63 us (36%)
  starting transfers between devices  8 us (33%)
  Pallas kernels  5.9 us (24%)
  waiting for transfers between devices  1.29 us (5%)
    all_to_all x1, blocking collectives, shards(): lax.all_to_all(half, ('band', 'blk'), split_axis=0, concat_axis=0, tiled=...  8.63 us
    all_to_all x1, starting transfers between devices, shards(): lax.all_to_all(sent, 'blk', split_axis=0, concat_axis=0, tiled=True, axis...  7.77 us
    pallas_call x1, Pallas kernels, shards(): pl.pallas_call(functools.partial(synth_kernel, blks, bands), out_shape=[j...  2.18 us
    pallas_call x1, Pallas kernels, shards(): pl.pallas_call(gram_kernel, out_shape=[jax.ShapeDtypeStruct((rows, 4 * ro...  1.99 us
    pallas_call x1, Pallas kernels, shards(): pl.pallas_call(functools.partial(analysis_kernel, bands), out_shape=jax.S...  1.25 us
    ppermute x1, waiting for transfers between devices, shards(): got = lax.ppermute(give, 'blk', [(k, k ^ 1) for k in range(blks)])  0.84 us
  transfers between devices with their start and end apart: 2, of which 2 were waited for; matrix products, arithmetic and copies ran while one was open for 0% of the time, Pallas kernels for 9%

profile of v10, /device:TPU:0, one launch (start us, length us, event | category | flops | bytes accessed | tf_op | source)
XLA Modules:
  0.0 23.9 jit_solution(13625845965643578997)
XLA Ops:
  0.0 2.2 %shard_map.73 = (f32[128,128]{1,0:T(8,128)}, s32[16]{0:T(128)S(1)}, s32[64]{0:T(128)S(1)}, s32[64]{0:T(128)S(1)}, f32[4,4096]{1,0:T(4,128)S(1)}, /*index=5*/f32[16,128]{1,0:T(8,128)S(1)}) custom-call(bf16[2560,128]{1,0:T(8,128)(2,1)} %bitcast.21, f32[1,2560]{1,0:T(1,128)} %beam_hbm.1, bf16[64,2560]{1,0:T(8,128)(2,1)} %bitcast.19, s32[16]{0:T(128)} %order_hbm.1, ...), custom_call_target="tpu_custom_call" | custom-call | flops 41943040000 | tf_op jit(solution)/shard_map/pallas_call | solution.py:301
  2.2 7.8 %all-to-all-start = ((f32[16,8,128]{2,1,0:T(8,128)}), f32[16,8,128]{2,1,0:T(8,128)S(1)}, u32[]{:S(2)}, u32[]{:S(2)}) async-start(f32[16,8,128]{2,1,0:T(8,128)} %bitcast.20), calls=%async_computation | async-start | bytes 131072 | tf_op jit(solution)/shard_map/all_to_all | solution.py:327
  10.0 0.0 copy-start
  10.0 2.0 %shard_map.74 = (bf16[64,256]{1,0:T(8,128)(2,1)S(1)}, bf16[64,256]{1,0:T(8,128)(2,1)S(1)}) custom-call(s32[16]{0:T(128)S(1)} %get-tuple-element.15.order_ref, s32[64]{0:T(128)S(1)} %get-tuple-element.16.cycle_ref, s32[64]{0:T(128)S(1)} %get-tuple-element.17.count_ref, f32[4,4096]{1,0:T(4,128)S(1)} %get-tuple-element.18.noise_ref), custom_call_target="tpu_custom_call" | custom-call | flops 268435456 | bytes 2097152 | tf_op jit(solution)/shard_map/pallas_call | solution.py:331
  12.0 0.2 collective-permute-start
  12.2 0.0 copy-done
  12.2 0.2 shard_map.76.leg_ref
  12.4 0.8 %collective-permute-done.got_ref = bf16[64,256]{1,0:T(8,128)(2,1)S(1)} collective-permute-done((bf16[64,256]{1,0:T(8,128)(2,1)S(1)}, bf16[64,256]{1,0:T(8,128)(2,1)S(1)}, u32[]{:S(2)}, u32[]{:S(2)}) %collective-permute-start) | collective-permute-done | bytes 32800 | tf_op jit(solution)/shard_map/ppermute | solution.py:343
  13.2 0.4 %all-to-all-done = f32[16,8,128]{2,1,0:T(8,128)S(1)} async-done(((f32[16,8,128]{2,1,0:T(8,128)}), f32[16,8,128]{2,1,0:T(8,128)S(1)}, u32[]{:S(2)}, u32[]{:S(2)}) %all-to-all-start) | async-done | bytes 65568 | tf_op jit(solution)/shard_map/all_to_all | solution.py:327
  13.7 0.3 %shard_map.75 = bf16[256,128]{1,0:T(8,128)(2,1)S(1)} custom-call(bf16[64,256]{1,0:T(8,128)(2,1)S(1)} %get-tuple-element.19.keep_ref, bf16[64,256]{1,0:T(8,128)(2,1)S(1)} %collective-permute-done.got_ref, f32[128,128]{1,0:T(8,128)S(1)} %bitcast.16, f32[16,128]{1,0:T(8,128)S(1)} %get-tuple-element.22.extra_ref), custom_call_target="tpu_custom_call" | custom-call | tf_op jit(solution)/shard_map/pallas_call | solution.py:355
  14.0 8.6 %all_to_all.22 = bf16[16,16,128]{2,1,0:T(8,128)(2,1)S(1)} all-to-all(bf16[16,16,128]{2,1,0:T(8,128)(2,1)S(1)} %bitcast.17), channel_id=1, replica_groups={{27,11,25,9,31,15,29,13,22,6,20,4,18,2,16,0},{26,10,24,8,30,14,28,12,23..., dimensions={0} | all-to-all | bytes 131072 | tf_op jit(solution)/shard_map/all_to_all | solution.py:368
  22.6 1.2 %shard_map.77 = f32[1280,128]{1,0:T(8,128)} custom-call(bf16[1280,64]{1,0:T(8,128)(2,1)S(1)} %shard_map.76.leg_ref, bf16[256,128]{1,0:T(8,128)(2,1)S(1)} %bitcast.18), custom_call_target="tpu_custom_call" | custom-call | tf_op jit(solution)/shard_map/pallas_call | solution.py:372
  (1 shorter events, 0.0 us)
Async XLA Ops:
  2.2 11.5 %all-to-all-start = ((f32[16,8,128]{2,1,0:T(8,128)}), f32[16,8,128]{2,1,0:T(8,128)S(1)}, u32[]{:S(2)}, u32[]{:S(2)}) async-start(f32[16,8,128]{2,1,0:T(8,128)} %bitcast.20), calls=%async_computation | async-start | bytes 131072 | tf_op jit(solution)/shard_map/all_to_all | solution.py:327
  10.0 2.2 %copy-start = (bf16[1,2560,64]{1,2,0:T(8,128)(2,1)S(1)}, bf16[1,2560,64]{1,2,0:T(8,128)(2,1)}, u32[]{:S(2)}) copy-start(bf16[1,2560,64]{1,2,0:T(8,128)(2,1)} %param.9) | copy-start | bytes 983044
  12.0 1.3 %collective-permute-start = (bf16[64,256]{1,0:T(8,128)(2,1)S(1)}, bf16[64,256]{1,0:T(8,128)(2,1)S(1)}, u32[]{:S(2)}, u32[]{:S(2)}) collective-permute-start(bf16[64,256]{1,0:T(8,128)(2,1)S(1)} %get-tuple-element.20), channel_id=1, source_target_pairs={{0,1},{1,0},{2,3},{3,2},{4,5},{5,4},{6,7},{7,6},{8,9},{9,8},{10,11... | collective-permute-start | bytes 98312 | tf_op jit(solution)/shard_map/ppermute | solution.py:343
